TPU v7x, 256 devices: a whole 4x4x8 slice. The times are simulated.
256 devices in a mesh: ctx: 64 (over y, z, core), head: 4 (over x).
Axes of the slice: x: 4, y: 4, z: 8, core: 2. Of those that a mesh axis runs over, the one named last changes fastest.
Arguments:
- queries: bfloat16 [32768, 4096], P('ctx', 'head'), may hold values from -25 to 25
- key_rows: bfloat16 [32768, 4096], P('ctx', 'head'), may hold values from -6 to 6
- value_rows: bfloat16 [32768, 4096], P('ctx', 'head'), may hold values from -6 to 6
- norm_gain: float32 [4096], P('head'), may hold values from 0.5 to 1.5
- cotangent: bfloat16 [32768, 4096], P('ctx', 'head'), may hold values from -6 to 6
Outputs:
- normed: bfloat16 [32768, 4096], P('ctx', 'head')
- grad_queries: bfloat16 [32768, 4096], P('ctx', 'head')
- grad_keys: bfloat16 [32768, 4096], P('ctx', 'head')
- grad_values: bfloat16 [32768, 4096], P('ctx', 'head')
All inputs are finite; a program needn't handle non-finite values.
Results may differ from a plain program's by a relative error of at most 0.015.
Values may be sent and summed in bfloat16 or wider, within the bound.
A program may use at most 192 MiB of HBM per device.

v0:
```python
import jax
import jax.numpy as jnp
from jax import lax
from jax.sharding import PartitionSpec as P

DH = 128


def prefix_2(value, axis, join, neutral, backward):
    count = lax.axis_size(axis)
    place = lax.axis_index(axis)
    ahead = count - 1 - place if backward else place
    gathered = lax.all_gather(value.astype(jnp.bfloat16), axis)
    state = jnp.zeros_like(value) + jnp.asarray(neutral, value.dtype)

    def one(step, state):
        source = count - 1 - step if backward else step
        return join(state, lax.dynamic_index_in_dim(gathered, source, 0, False).astype(value.dtype))

    return lax.fori_loop(0, ahead, one, state)


def add_states(earlier, later_one):
    return earlier + later_one


def per_device(queries, key_rows, value_rows, norm_gain, cotangent):
    tok_count, local_width = queries.shape
    head_count = local_width // DH
    query3 = queries.reshape(tok_count, head_count, DH)
    key3 = key_rows.reshape(tok_count, head_count, DH)
    value3 = value_rows.reshape(tok_count, head_count, DH)
    causal = jnp.tril(jnp.ones((tok_count, tok_count), dtype=jnp.bool_))
    local_state = jnp.einsum("shd,she->hde", key3, value3, preferred_element_type=jnp.float32)
    zero_state = jnp.zeros_like(local_state)
    prefix = prefix_2(local_state, "ctx", add_states, zero_state, False)
    prefix_low = prefix.astype(jnp.bfloat16)
    scores = jnp.einsum("thd,shd->hts", query3, key3, preferred_element_type=jnp.float32) / DH
    weights = jnp.where(causal[None], scores, jnp.float32(0.0)).astype(jnp.bfloat16)
    attended = jnp.einsum("hts,she->the", weights, value3, preferred_element_type=jnp.float32)
    attended = (
        attended
        + jnp.einsum("thd,hde->the", query3, prefix_low, preferred_element_type=jnp.float32) / DH
    )
    attended = attended.reshape(tok_count, local_width)
    full_width = local_width * lax.axis_size("head")
    squares = lax.psum(jnp.sum(attended * attended, axis=1), "head")
    radius = jnp.sqrt(squares / full_width + 1e-06)
    normed = (norm_gain * attended / radius[:, None]).astype(jnp.bfloat16)
    scaled = norm_gain * cotangent.astype(jnp.float32)
    inner = lax.psum(jnp.sum(attended * scaled, axis=1), "head")
    factor = inner / (full_width * radius * radius)
    grad_out = ((scaled - attended * factor[:, None]) / radius[:, None]).astype(jnp.bfloat16)
    grad3 = grad_out.reshape(tok_count, head_count, DH)
    grad_state = jnp.einsum("thd,the->hde", query3, grad3, preferred_element_type=jnp.float32)
    suffix = prefix_2(grad_state, "ctx", add_states, zero_state, True)
    suffix_low = suffix.astype(jnp.bfloat16)
    grad_scores = jnp.einsum("the,she->hts", grad3, value3, preferred_element_type=jnp.float32) / DH
    grad_weights = jnp.where(causal[None], grad_scores, jnp.float32(0.0)).astype(jnp.bfloat16)
    grad_query = jnp.einsum("hts,shd->thd", grad_weights, key3, preferred_element_type=jnp.float32)
    grad_query = (
        grad_query
        + jnp.einsum("the,hde->thd", grad3, prefix_low, preferred_element_type=jnp.float32) / DH
    )
    grad_key = jnp.einsum("hts,thd->shd", grad_weights, query3, preferred_element_type=jnp.float32)
    grad_key = (
        grad_key
        + jnp.einsum("she,hde->shd", value3, suffix_low, preferred_element_type=jnp.float32) / DH
    )
    grad_value = jnp.einsum("hts,the->she", weights, grad3, preferred_element_type=jnp.float32)
    grad_value = (
        grad_value
        + jnp.einsum("shd,hde->she", key3, suffix_low, preferred_element_type=jnp.float32) / DH
    )
    return (
        normed,
        grad_query.reshape(tok_count, local_width).astype(jnp.bfloat16),
        grad_key.reshape(tok_count, local_width).astype(jnp.bfloat16),
        grad_value.reshape(tok_count, local_width).astype(jnp.bfloat16),
    )


def solution(mesh):
    placed = (P("ctx", "head"), P("ctx", "head"), P("ctx", "head"), P("head"), P("ctx", "head"))
    return jax.shard_map(
        per_device,
        mesh=mesh,
        in_specs=placed,
        out_specs=(P("ctx", "head"), P("ctx", "head"), P("ctx", "head"), P("ctx", "head")),
        check_vma=False,
    )
```

profile of v0, /device:TPU:1, one launch (start us, length us, event | category | flops | bytes accessed | tf_op | source)
XLA Modules:
  0.0 393.8 jit_solution(13908855633397536914)
XLA Ops:
  7.2 1.6 copy.65
  8.8 1.5 copy.37
  10.3 2.5 convolution_convert_fusion.1
  12.9 3.3 select_convert_fusion.1
  16.3 100.8 %all-gather.5.cloned.1.call-done = bf16[512,128,128]{2,1,0:T(8,128)(2,1)} async-done(((bf16[8,128,128]{2,1,0:T(8,128)(2,1)}), bf16[512,128,128]{2,1,0:T(8,128)(2,1)}) %all-gather.5.cloned.1.call-update) | async-done | bytes 16777232 | tf_op jit(solution)/shard_map/all_gather | solution.py:13
  117.1 1.2 while.22
  117.1 1.2 convert_add_fusion.4
  118.9 5.1 %multiply_reduce_fusion.1 = (f32[512]{0:T(512)S(1)}, f32[512,8,128]{0,2,1:T(8,128)}) fusion(f32[8,128,512]{2,1,0:T(8,128)S(1)} %fusion.13, bf16[8,512,512]{2,1,0:T(8,128)(2,1)} %select_convert_fusion.1, bf16[512,1024]{1,0:T(8,128)(2,1)S(1)} %copy-done), kind=kOutput, calls=%fused_computation.14 | convolution fusion | flops 538967552 | bytes 9439232 | tf_op jit(solution)/shard_map/hts,she->the/dot_general | solution.py:40
  123.9 3.0 copy.41
  126.9 1.9 multiply_reduce_fusion
  128.9 8.4 %all-reduce = (f32[512]{0:T(512)S(1)}, f32[512]{0:T(512)S(1)}) all-reduce(f32[512]{0:T(512)S(1)} %get-tuple-element.119, f32[512]{0:T(512)S(1)} %multiply_reduce_fusion), channel_id=1, replica_groups=mesh['ctx'=64,'head'=4] {'head'}, use_global_device_ids=true, to_apply=%region_3.4 | all-reduce | flops 1024 | bytes 8192 | tf_op jit(solution)/shard_map/psum | solution.py:47
  137.3 3.5 divide_convert_fusion
  140.8 1.5 copy.61
  142.3 1.7 fusion.2
  145.3 1.5 select_convert_fusion
  146.9 2.5 fusion.1
  149.3 2.3 copy.56
  151.6 4.3 %fusion.31 = f32[8,128,512]{2,1,0:T(8,128)} fusion(bf16[512,8,128]{0,2,1:T(8,128)(2,1)S(1)} %bitcast.110, bf16[8,512,512]{2,1,0:T(8,128)(2,1)} %select_convert_fusion.1), kind=kOutput, calls=%fused_computation.49 | convolution fusion | flops 536870912 | bytes 7340032 | tf_op jit(solution)/shard_map/hts,the->she/dot_general | solution.py:70
  155.9 150.2 %all-gather.7.cloned.1.call-done = bf16[512,128,128]{2,1,0:T(8,128)(2,1)} async-done(((bf16[8,128,128]{2,1,0:T(8,128)(2,1)}), bf16[512,128,128]{2,1,0:T(8,128)(2,1)}) %all-gather.7.cloned.1.call-update) | async-done | bytes 16777232 | tf_op jit(solution)/shard_map/all_gather | solution.py:13
  306.1 67.7 %while.23 = (s32[]{:T(128)}, f32[8,128,128]{2,1,0:T(8,128)S(1)}, s32[]{:T(128)}, bf16[64,8,128,128]{3,2,1,0:T(8,128)(2,1)}, s32[]{:T(128)}, /*index=5*/s32[]{:T(128)}, s32[]{:T(128)}, s32[]{:T(128)}) while((s32[]{:T(128)}, f32[8,128,128]{2,1,0:T(8,128)S(1)}, s32[]{:T(128)}, bf16[64,8,128,128]{3,2,1,0:T(8,128)(2,1)}, s32[]{:T(128)}, ...), condition=%wide.region_7.8_spmd, body=%wide.region_6.7_spmd.sunk | while | flops 262150 | bytes 1310863 | solution.py:20
  306.1 1.1 convert_add_fusion.5
  307.2 1.1 convert_add_fusion.5
  309.4 1.1 convert_add_fusion.5
  310.5 1.1 convert_add_fusion.5
  313.8 1.1 convert_add_fusion.5
  314.9 1.1 convert_add_fusion.5
  317.0 1.1 convert_add_fusion.5
  373.8 1.8 fusion.4
  376.4 1.5 add_convert_fusion
  377.9 2.4 copy.58
  380.4 4.3 %fusion = bf16[512,8,128]{0,2,1:T(8,128)(2,1)} fusion(f32[8,128,512]{2,1,0:T(8,128)S(1)} %copy-done.3, bf16[8,512,512]{2,1,0:T(8,128)(2,1)} %copy-done.1, bf16[512,1024]{1,0:T(8,128)(2,1)} %param.9), kind=kOutput, calls=%fused_computation.5 | convolution fusion | flops 538443776 | bytes 8388608 | tf_op jit(solution)/shard_map/hts,thd->shd/dot_general | solution.py:65
  384.7 2.3 copy.57
  (88 shorter events, 61.8 us)
Async XLA Ops:
  7.2 3.1 copy-start
  7.2 109.9 %all-gather.5.cloned.1.call-start = ((), (), s32[]{:S(2)}) async-start(), calls=%async_computation | async-start | bytes 17039360 | tf_op jit(solution)/shard_map/all_gather | solution.py:13
  8.8 4.1 %copy-start.5 = (bf16[512,1024]{1,0:T(8,128)(2,1)S(1)}, bf16[512,1024]{1,0:T(8,128)(2,1)}, u32[]{:S(2)}) copy-start(bf16[512,1024]{1,0:T(8,128)(2,1)} %param.10) | copy-start | bytes 3145732
  10.3 2.6 copy-start.7
  12.8 293.3 %all-gather.7.cloned.1.call-start = ((), (), s32[]{:S(2)}) async-start(), calls=%async_computation.1 | async-start | bytes 17039360 | tf_op jit(solution)/shard_map/all_gather | solution.py:13
  117.1 1.3 copy-start.8
  123.9 3.0 copy-start.4
  123.9 3.0 copy-start.10
  145.3 1.5 copy-start.9
  146.9 2.5 copy-start.1
  373.8 1.9 copy-start.2
  373.8 2.6 copy-start.6
  377.9 2.4 copy-start.3
Sparse Core Ops, SparseCore 0:
  12.9 104.1 all-gather.4
  145.0 161.0 all-gather.6
where the time goes:
time: 396 us; the launch traced here: 394 us
  waiting for transfers between devices  251 us (63%)
  other arithmetic  73 us (18%)
  matrix products  29.3 us (7%)
  local copies, waits for them, and re-layouts  16.3 us (4%)
  between operations  14.2 us (4%)
  blocking collectives  8.41 us (2%)
    all_gather x2, waiting for transfers between devices, prefix_2(): gathered = lax.all_gather(value.astype(jnp.bfloat16), axis)  251 us
    add x63, other arithmetic, add_states(): return earlier + later_one  67.5 us
    unnamed x26, local copies, waits for them, and re-layouts  9.47 us
    psum x1, blocking collectives, per_device(): squares = lax.psum(jnp.sum(attended * attended, axis=1), 'head')  8.41 us
  transfers between devices with their start and end apart: 2, of which 2 were waited for; matrix products, arithmetic and copies ran while one was open for 4% of the time, Pallas kernels for 0%

commit v1 on v0

v1 whole, which is shorter than its diff:
```python
import functools

import jax
import jax.numpy as jnp
from jax import lax
from jax.experimental import pallas as pl
from jax.experimental.pallas import tpu as pltpu
from jax.sharding import PartitionSpec as P

MESH = pl.DeviceIdType.MESH
F32 = jnp.float32
BF16 = jnp.bfloat16
DH = 128
TOK = 512
HEADS = 8
WIDTH = HEADS * DH
HALF = HEADS // 2 * DH
NY, NZ, NX = 4, 8, 4
CHIPS = NY * NZ
PIECE = HALF // CHIPS
FULL_WIDTH = WIDTH * NX
CUT = TOK // 2


def far_first():
    def reach(offset):
        return min(offset[0], NY - offset[0]) + min(offset[1], NZ - offset[1])

    offsets = [(dy, dz) for dy in range(NY) for dz in range(NZ) if dy or dz]
    return sorted(offsets, key=lambda offset: -reach(offset))


def nn(a, b):
    return lax.dot_general(a, b, (((1,), (0,)), ((), ())), preferred_element_type=F32)


def nt(a, b):
    return lax.dot_general(a, b, (((1,), (1,)), ((), ())), preferred_element_type=F32)


def tn(a, b):
    return lax.dot_general(a, b, (((0,), (0,)), ((), ())), preferred_element_type=F32)


def await_bytes(ref, sem):
    pltpu.make_async_copy(ref, ref, sem).wait()


def kernel(
    q_hbm,
    k_hbm,
    v_hbm,
    gain_hbm,
    c_hbm,
    normed,
    grad_q,
    grad_k,
    grad_v,
    q,
    k,
    v,
    gain,
    c,
    q8,
    g,
    w,
    att,
    part_k,
    part_v,
    inv_ref,
    fac_ref,
    state_own,
    state_out,
    state_in,
    chip_sum,
    owned,
    scanned,
    chip_scan,
    scan_out,
    scan,
    stats,
    load_sem,
    send_sem,
    recv_sem,
):
    place = lax.axis_index("ctx")
    hx = lax.axis_index("head")
    chip = lax.div(place, 2)
    core = lax.rem(place, 2)
    chip_y = lax.div(chip, NZ)
    chip_z = lax.rem(chip, NZ)
    sibling = (chip * 2 + 1 - core, hx)

    def chip_at(dy, dz):
        return lax.rem(chip_y + dy, NY) * NZ + lax.rem(chip_z + dz, NZ)

    offsets = far_first()
    barrier = pltpu.get_barrier_semaphore()

    def greet(device):
        pl.semaphore_signal(barrier, inc=1, device_id=device, device_id_type=MESH)

    for dy, dz in offsets:
        greet((chip_at(dy, dz) * 2 + core, hx))
    for step in range(1, NX):
        greet((place, lax.rem(hx + step, NX)))
    greet(sibling)

    loads = [
        pltpu.make_async_copy(src, dst, load_sem.at[n])
        for n, (src, dst) in enumerate(
            [(k_hbm, k), (v_hbm, v), (q_hbm, q), (gain_hbm, gain), (c_hbm, c)]
        )
    ]
    for load in loads:
        load.start()

    def columns(h):
        return pl.ds(pl.multiple_of(h * DH, DH), DH)

    def rows_of(h):
        return pl.ds(pl.multiple_of(h * DH, DH), DH)

    theirs = pl.multiple_of((1 - core) * HALF, HALF)
    ours = pl.multiple_of(core * HALF, HALF)

    def send(src, dst, n, device):
        pltpu.make_async_remote_copy(
            src_ref=src,
            dst_ref=dst,
            send_sem=send_sem.at[n],
            recv_sem=recv_sem.at[n],
            device_id=device,
            device_id_type=MESH,
        ).start()

    def scan_begin(s, local_state, first):
        def give(i, carry):
            state_out[s, rows_of(i), :] = local_state((1 - core) * (HEADS // 2) + i).astype(BF16)
            return carry

        lax.fori_loop(0, HEADS // 2, give, 0)
        if first:
            pl.semaphore_wait(barrier, len(offsets) + NX)
        send(state_out.at[s], state_in.at[s], 4 * s, sibling)

        def keep(i, carry):
            state_own[s, rows_of(i), :] = local_state(core * (HEADS // 2) + i)
            return carry

        lax.fori_loop(0, HEADS // 2, keep, 0)
        await_bytes(state_in.at[s], recv_sem.at[4 * s])
        both = state_own[s] + state_in[s].astype(F32)
        chip_sum[s] = both.astype(BF16).reshape(CHIPS, PIECE, DH)
        for dy, dz in offsets:
            other = chip_at(dy, dz)
            send(chip_sum.at[s, other], owned.at[s, chip], 4 * s + 1, (other * 2 + core, hx))
        owned[s, chip] = chip_sum[s, chip]

    def scan_middle(s, backward):
        await_bytes(owned.at[s, pl.ds(0, CHIPS - 1)], recv_sem.at[4 * s + 1])
        total = jnp.zeros((PIECE, DH), F32)
        for n in range(CHIPS):
            one = CHIPS - 1 - n if backward else n
            scanned[s, one] = total.astype(BF16)
            total = total + owned[s, one].astype(F32)
        for dy, dz in offsets:
            other = chip_at(dy, dz)
            send(scanned.at[s, other], chip_scan.at[s, chip], 4 * s + 2, (other * 2 + core, hx))
        chip_scan[s, chip] = scanned[s, chip]

    def scan_end(s, backward, scale):
        await_bytes(chip_scan.at[s, pl.ds(0, CHIPS - 1)], recv_sem.at[4 * s + 2])
        ahead = chip_scan[s].astype(F32).reshape(HALF, DH)
        leads = core == (1 if backward else 0)
        give = ahead + jnp.where(leads, state_own[s], 0.0)
        scan_out[s] = (give * scale).astype(BF16)
        send(scan_out.at[s], scan.at[s, pl.ds(ours, HALF)], 4 * s + 3, sibling)
        keep = ahead + jnp.where(leads, 0.0, state_in[s].astype(F32))
        scan[s, pl.ds(ours, HALF), :] = (keep * scale).astype(BF16)
        await_bytes(scan_out.at[s], recv_sem.at[4 * s + 3])

    row_at = lax.broadcasted_iota(jnp.int32, (CUT, CUT), 0)
    col_at = lax.broadcasted_iota(jnp.int32, (CUT, CUT), 1)
    causal = col_at <= row_at

    def lower(scores):
        return jnp.where(causal, scores, 0.0).astype(BF16)

    loads[0].wait()
    loads[1].wait()
    scan_begin(0, lambda h: tn(k[:, columns(h)], v[:, columns(h)]), True)
    for load in loads[2:]:
        load.wait()

    def inside(h, carry):
        col = columns(h)
        q8_h = q[:, col] * jnp.asarray(1.0 / DH, BF16)
        q8[:, col] = q8_h
        k_h, v_h = k[:, col], v[:, col]
        w00 = lower(nt(q8_h[:CUT], k_h[:CUT]))
        w[h, :CUT, :CUT] = w00
        att[:CUT, col] = nn(w00, v_h[:CUT])
        w10 = nt(q8_h[CUT:], k_h[:CUT]).astype(BF16)
        w11 = lower(nt(q8_h[CUT:], k_h[CUT:]))
        w[h, CUT:, :CUT] = w10
        w[h, CUT:, CUT:] = w11
        att[CUT:, col] = nn(w10, v_h[:CUT]) + nn(w11, v_h[CUT:])
        return carry

    lax.fori_loop(0, HEADS // 2, inside, 0)
    scan_middle(0, False)
    lax.fori_loop(HEADS // 2, HEADS, inside, 0)
    scan_end(0, False, 1.0)

    def across(h, carry):
        col = columns(h)
        att[:, col] += nn(q8[:, col], scan[0, rows_of(h), :])
        return carry

    lax.fori_loop(0, HEADS, across, 0)

    def row_sums(b, carry):
        rows = pl.ds(pl.multiple_of(b * DH, DH), DH)
        squares = jnp.zeros((DH, DH), F32)
        inner = jnp.zeros((DH, DH), F32)
        for h in range(HEADS):
            col = slice(h * DH, (h + 1) * DH)
            a = att[rows, col]
            squares += a * a
            inner += a * (gain[:, col] * c[rows, col].astype(F32))
        stats[hx, 0:1, rows] = jnp.sum(squares.T, axis=0, keepdims=True)
        stats[hx, 1:2, rows] = jnp.sum(inner.T, axis=0, keepdims=True)
        return carry

    lax.fori_loop(0, TOK // DH, row_sums, 0)
    for step in range(1, NX):
        send(stats.at[hx], stats.at[hx], 8, (place, lax.rem(hx + step, NX)))
    await_bytes(stats.at[pl.ds(0, NX - 1)], recv_sem.at[8])
    sums = stats[0] + stats[1] + stats[2] + stats[3]
    mean_square = sums[0:1] * (1.0 / FULL_WIDTH) + 1e-6
    inverse = 1.0 / jnp.sqrt(mean_square)
    factor = sums[1:2] / (FULL_WIDTH * mean_square)
    for b in range(TOK // DH):
        rows = slice(b * DH, (b + 1) * DH)
        inv_ref[rows, :] = jnp.broadcast_to(inverse[:, rows], (DH, DH)).T
        fac_ref[rows, :] = jnp.broadcast_to(factor[:, rows], (DH, DH)).T

    def gradient_state(h):
        col = columns(h)
        scaled = gain[:, col] * c[:, col].astype(F32)
        g_h = ((scaled - att[:, col] * fac_ref[...]) * inv_ref[...]).astype(BF16)
        g[:, col] = g_h
        return tn(q[:, col], g_h)

    scan_begin(1, gradient_state, False)

    def inside_back(h, carry):
        col = columns(h)
        normed[:, col] = (gain[:, col] * att[:, col] * inv_ref[...]).astype(BF16)
        q_h, k_h, v_h, g_h = q[:, col], k[:, col], v[:, col], g[:, col]
        g8 = g_h * jnp.asarray(1.0 / DH, BF16)
        before = scan[0, rows_of(h), :]
        u00 = lower(nt(g8[:CUT], v_h[:CUT]))
        u10 = nt(g8[CUT:], v_h[:CUT]).astype(BF16)
        u11 = lower(nt(g8[CUT:], v_h[CUT:]))
        grad_q[:CUT, col] = (nn(u00, k_h[:CUT]) + nt(g8[:CUT], before)).astype(BF16)
        grad_q[CUT:, col] = (
            nn(u10, k_h[:CUT]) + nn(u11, k_h[CUT:]) + nt(g8[CUT:], before)
        ).astype(BF16)
        part_k[:CUT, col] = tn(u00, q_h[:CUT]) + tn(u10, q_h[CUT:])
        part_k[CUT:, col] = tn(u11, q_h[CUT:])
        part_v[:CUT, col] = tn(w[h, :CUT, :CUT], g_h[:CUT]) + tn(w[h, CUT:, :CUT], g_h[CUT:])
        part_v[CUT:, col] = tn(w[h, CUT:, CUT:], g_h[CUT:])
        return carry

    lax.fori_loop(0, HEADS // 2, inside_back, 0)
    scan_middle(1, True)
    lax.fori_loop(HEADS // 2, HEADS, inside_back, 0)
    scan_end(1, True, 1.0 / DH)

    def last(h, carry):
        col = columns(h)
        after = scan[1, rows_of(h), :]
        grad_k[:, col] = (part_k[:, col] + nt(v[:, col], after)).astype(BF16)
        grad_v[:, col] = (part_v[:, col] + nn(k[:, col], after)).astype(BF16)
        return carry

    lax.fori_loop(0, HEADS, last, 0)

    for s in range(2):
        await_bytes(state_out.at[s], send_sem.at[4 * s])
        await_bytes(chip_sum.at[s, pl.ds(0, CHIPS - 1)], send_sem.at[4 * s + 1])
        await_bytes(scanned.at[s, pl.ds(0, CHIPS - 1)], send_sem.at[4 * s + 2])
        await_bytes(scan_out.at[s], send_sem.at[4 * s + 3])
    await_bytes(stats.at[pl.ds(0, NX - 1)], send_sem.at[8])


def per_device(queries, key_rows, value_rows, norm_gain, cotangent):
    block = jax.ShapeDtypeStruct((TOK, WIDTH), BF16)
    held = pltpu.VMEM((TOK, WIDTH), BF16)
    held32 = pltpu.VMEM((TOK, WIDTH), F32)
    half = pltpu.VMEM((2, HALF, DH), BF16)
    pieces = pltpu.VMEM((2, CHIPS, PIECE, DH), BF16)
    return pl.pallas_call(
        kernel,
        out_shape=[block] * 4,
        in_specs=[pl.BlockSpec(memory_space=pltpu.HBM)] * 5,
        out_specs=[pl.BlockSpec(memory_space=pltpu.VMEM)] * 4,
        scratch_shapes=[
            held,
            held,
            held,
            pltpu.VMEM((1, WIDTH), F32),
            held,
            held,
            held,
            pltpu.VMEM((HEADS, TOK, TOK), BF16),
            held32,
            held32,
            held32,
            pltpu.VMEM((TOK, DH), F32),
            pltpu.VMEM((TOK, DH), F32),
            pltpu.VMEM((2, HALF, DH), F32),
            half,
            half,
            pieces,
            pieces,
            pieces,
            pieces,
            half,
            pltpu.VMEM((2, 2 * HALF, DH), BF16),
            pltpu.VMEM((NX, 2, TOK), F32),
            pltpu.SemaphoreType.DMA((5,)),
            pltpu.SemaphoreType.DMA((9,)),
            pltpu.SemaphoreType.DMA((9,)),
        ],
        compiler_params=pltpu.CompilerParams(
            collective_id=0, has_side_effects=True, vmem_limit_bytes=40 << 20
        ),
    )(queries, key_rows, value_rows, norm_gain.reshape(1, WIDTH), cotangent)


def solution(mesh):
    placed = (P("ctx", "head"), P("ctx", "head"), P("ctx", "head"), P("head"), P("ctx", "head"))
    return jax.shard_map(
        per_device,
        mesh=mesh,
        in_specs=placed,
        out_specs=(P("ctx", "head"), P("ctx", "head"), P("ctx", "head"), P("ctx", "head")),
        check_vma=False,
    )
```

time: 396 us -> 60.4 us (0.15)
  waiting for transfers between devices: 251 us -> 0 us
  other arithmetic: 73 us -> 0 us
  Pallas kernels: 0 us -> 50 us
  matrix products: 29.3 us -> 0 us
  between operations: 14.2 us -> 0.65 us
  blocking collectives: 8.41 us -> 0 us
  local copies, waits for them, and re-layouts: 16.3 us -> 9.46 us
    all_gather x2 -> x0, waiting for transfers between devices: 251 us -> none  [prefix_2(): gathered = lax.all_gather(value.astype(jnp.bfloat16), axis)]
    add x63 -> x0, other arithmetic: 67.5 us -> none  [add_states(): return earlier + later_one]
    pallas_call x0 -> x1, Pallas kernels: none -> 50 us  [per_device(): pl.pallas_call(kernel, out_shape=[block] * 4, in_specs=[pl.BlockSpec(memo...]
    dot_general x12 -> x0, matrix products: 29.3 us -> none  [the longest x1 5.05 us: per_device(): jnp.einsum('hts,she->the', weights, value3, preferred_element_type=jnp.fl...]
    psum x1 -> x0, blocking collectives: 8.41 us -> none  [per_device(): squares = lax.psum(jnp.sum(attended * attended, axis=1), 'head')]
    reshape x3 -> x0, local copies, waits for them, and re-layouts: 5.94 us -> none  [the longest x1 2.99 us: per_device(): attended = attended.reshape(tok_count, local_width)]
    unnamed x26 -> x14, local copies, waits for them, and re-layouts: 9.47 us -> 9.46 us
  transfers between devices with their start and end apart: 2 -> 0, of which waited for: 2 -> 0; matrix products, arithmetic and copies ran while one was open for 4% -> 0% of each run, Pallas kernels for 0% -> 0%
where the time goes in v1:
time: 60.4 us; the launch traced here: 60.1 us
  Pallas kernels  50 us (83%)
  local copies, waits for them, and re-layouts  9.46 us (16%)
  between operations  0.65 us (1%)
    pallas_call x1, Pallas kernels, per_device(): pl.pallas_call(kernel, out_shape=[block] * 4, in_specs=[pl.BlockSpec(memo...  50 us
    unnamed x14, local copies, waits for them, and re-layouts  9.46 us

profile of v1, /device:TPU:1, one launch (start us, length us, event | category | flops | bytes accessed | tf_op | source)
XLA Modules:
  0.0 60.1 jit_solution(1023584879905203805)
XLA Ops:
  0.6 0.0 copy-start
  0.6 1.2 %copy-done = bf16[512,1024]{1,0:T(8,128)(2,1)S(1)} copy-done((bf16[512,1024]{1,0:T(8,128)(2,1)S(1)}, bf16[512,1024]{1,0:T(8,128)(2,1)}, u32[]{:S(2)}) %copy-start) | copy-done | bytes 1048600
  1.9 0.0 copy-start.1
  1.9 1.2 %copy-done.1 = bf16[512,1024]{1,0:T(8,128)(2,1)S(1)} copy-done((bf16[512,1024]{1,0:T(8,128)(2,1)S(1)}, bf16[512,1024]{1,0:T(8,128)(2,1)}, u32[]{:S(2)}) %copy-start.1) | copy-done | bytes 1048600
  3.1 0.0 copy-start.2
  3.1 1.2 %copy-done.2 = bf16[512,1024]{1,0:T(8,128)(2,1)S(1)} copy-done((bf16[512,1024]{1,0:T(8,128)(2,1)S(1)}, bf16[512,1024]{1,0:T(8,128)(2,1)}, u32[]{:S(2)}) %copy-start.2) | copy-done | bytes 1048600
  4.3 0.0 copy-start.3
  4.3 1.2 %copy-done.3 = bf16[512,1024]{1,0:T(8,128)(2,1)S(1)} copy-done((bf16[512,1024]{1,0:T(8,128)(2,1)S(1)}, bf16[512,1024]{1,0:T(8,128)(2,1)}, u32[]{:S(2)}) %copy-start.3) | copy-done | bytes 1048600
  5.5 0.0 copy-start.4
  5.5 0.7 %copy-done.4 = f32[1024]{0:T(1024)S(1)} copy-done((f32[1024]{0:T(1024)S(1)}, f32[1024]{0:T(1024)}, u32[]{:S(2)}) %copy-start.4) | copy-done | bytes 4120
  6.2 50.0 %shard_map.84 = (bf16[512,1024]{1,0:T(8,128)(2,1)S(1)}, bf16[512,1024]{1,0:T(8,128)(2,1)S(1)}, bf16[512,1024]{1,0:T(8,128)(2,1)S(1)}, bf16[512,1024]{1,0:T(8,128)(2,1)S(1)}) custom-call(bf16[512,1024]{1,0:T(8,128)(2,1)S(1)} %copy-done, bf16[512,1024]{1,0:T(8,128)(2,1)S(1)} %copy-done.1, bf16[512,1024]{1,0:T(8,128)(2,1)S(1)} %copy-done.2, ...), custom_call_target="tpu_custom_call" | custom-call | tf_op jit(solution)/shard_map/pallas_call | solution.py:305
  56.2 1.0 %copy.13 = bf16[512,1024]{1,0:T(8,128)(2,1)} copy(bf16[512,1024]{1,0:T(8,128)(2,1)S(1)} %get-tuple-element.8) | data formatting | bytes 2097152
  57.2 1.0 %copy.14 = bf16[512,1024]{1,0:T(8,128)(2,1)} copy(bf16[512,1024]{1,0:T(8,128)(2,1)S(1)} %get-tuple-element.9) | data formatting | bytes 2097152
  58.2 1.0 %copy.15 = bf16[512,1024]{1,0:T(8,128)(2,1)} copy(bf16[512,1024]{1,0:T(8,128)(2,1)S(1)} %get-tuple-element.10) | data formatting | bytes 2097152
  59.2 1.0 %copy.16 = bf16[512,1024]{1,0:T(8,128)(2,1)} copy(bf16[512,1024]{1,0:T(8,128)(2,1)S(1)} %get-tuple-element.11) | data formatting | bytes 2097152
Async XLA Ops:
  0.6 1.2 %copy-start = (bf16[512,1024]{1,0:T(8,128)(2,1)S(1)}, bf16[512,1024]{1,0:T(8,128)(2,1)}, u32[]{:S(2)}) copy-start(bf16[512,1024]{1,0:T(8,128)(2,1)} %q_hbm.1) | copy-start | bytes 3145732
  1.9 1.2 %copy-start.1 = (bf16[512,1024]{1,0:T(8,128)(2,1)S(1)}, bf16[512,1024]{1,0:T(8,128)(2,1)}, u32[]{:S(2)}) copy-start(bf16[512,1024]{1,0:T(8,128)(2,1)} %k_hbm.1) | copy-start | bytes 3145732
  3.1 1.2 %copy-start.2 = (bf16[512,1024]{1,0:T(8,128)(2,1)S(1)}, bf16[512,1024]{1,0:T(8,128)(2,1)}, u32[]{:S(2)}) copy-start(bf16[512,1024]{1,0:T(8,128)(2,1)} %v_hbm.1) | copy-start | bytes 3145732
  4.3 1.2 %copy-start.3 = (bf16[512,1024]{1,0:T(8,128)(2,1)S(1)}, bf16[512,1024]{1,0:T(8,128)(2,1)}, u32[]{:S(2)}) copy-start(bf16[512,1024]{1,0:T(8,128)(2,1)} %c_hbm.1) | copy-start | bytes 3145732
  5.5 0.7 %copy-start.4 = (f32[1024]{0:T(1024)S(1)}, f32[1024]{0:T(1024)}, u32[]{:S(2)}) copy-start(f32[1024]{0:T(1024)} %param.8) | copy-start | bytes 12292

commit v2 on v1

--- a/solution.py
+++ b/solution.py
@@ -54,19 +54,18 @@
     c_hbm,
     normed,
     grad_q,
-    grad_k,
-    grad_v,
-    q,
     k,
     v,
+    part_k,
+    part_v,
+    suffix,
+    q,
     gain,
     c,
     q8,
     g,
     w,
     att,
-    part_k,
-    part_v,
     inv_ref,
     fac_ref,
     state_own,
@@ -279,14 +278,7 @@
     lax.fori_loop(HEADS // 2, HEADS, inside_back, 0)
     scan_end(1, True, 1.0 / DH)
 
-    def last(h, carry):
-        col = columns(h)
-        after = scan[1, rows_of(h), :]
-        grad_k[:, col] = (part_k[:, col] + nt(v[:, col], after)).astype(BF16)
-        grad_v[:, col] = (part_v[:, col] + nn(k[:, col], after)).astype(BF16)
-        return carry
-
-    lax.fori_loop(0, HEADS, last, 0)
+    suffix[...] = scan[1]
 
     for s in range(2):
         await_bytes(state_out.at[s], send_sem.at[4 * s])
@@ -296,28 +288,52 @@
     await_bytes(stats.at[pl.ds(0, NX - 1)], send_sem.at[8])
 
 
+def finish(normed, grad_q, k, v, part_k, part_v, suffix, *rest):
+    normed_out, grad_q_out, grad_k_out, grad_v_out, grad_k, grad_v, sem = rest
+    stores = [
+        pltpu.make_async_copy(normed, normed_out, sem.at[0]),
+        pltpu.make_async_copy(grad_q, grad_q_out, sem.at[1]),
+    ]
+    for store in stores:
+        store.start()
+    for part in range(2):
+
+        def last(i, carry):
+            h = part * (HEADS // 2) + i
+            col = pl.ds(pl.multiple_of(h * DH, DH), DH)
+            after = suffix[col, :]
+            grad_k[:, col] = (part_k[:, col] + nt(v[:, col], after)).astype(BF16)
+            grad_v[:, col] = (part_v[:, col] + nn(k[:, col], after)).astype(BF16)
+            return carry
+
+        lax.fori_loop(0, HEADS // 2, last, 0)
+        some = pl.ds(part * HALF, HALF)
+        for n, (src, dst) in enumerate([(grad_k, grad_k_out), (grad_v, grad_v_out)]):
+            store = pltpu.make_async_copy(src.at[:, some], dst.at[:, some], sem.at[2 + 2 * part + n])
+            store.start()
+            stores.append(store)
+    for store in stores:
+        store.wait()
+
+
 def per_device(queries, key_rows, value_rows, norm_gain, cotangent):
     block = jax.ShapeDtypeStruct((TOK, WIDTH), BF16)
     held = pltpu.VMEM((TOK, WIDTH), BF16)
     held32 = pltpu.VMEM((TOK, WIDTH), F32)
     half = pltpu.VMEM((2, HALF, DH), BF16)
     pieces = pltpu.VMEM((2, CHIPS, PIECE, DH), BF16)
-    return pl.pallas_call(
+    passed = pl.pallas_call(
         kernel,
-        out_shape=[block] * 4,
+        out_shape=[held, held, held, held, held32, held32, pltpu.VMEM((WIDTH, DH), BF16)],
         in_specs=[pl.BlockSpec(memory_space=pltpu.HBM)] * 5,
-        out_specs=[pl.BlockSpec(memory_space=pltpu.VMEM)] * 4,
+        out_specs=[pl.BlockSpec(memory_space=pltpu.VMEM)] * 7,
         scratch_shapes=[
-            held,
-            held,
             held,
             pltpu.VMEM((1, WIDTH), F32),
             held,
             held,
             held,
             pltpu.VMEM((HEADS, TOK, TOK), BF16),
-            held32,
-            held32,
             held32,
             pltpu.VMEM((TOK, DH), F32),
             pltpu.VMEM((TOK, DH), F32),
@@ -336,9 +352,17 @@
             pltpu.SemaphoreType.DMA((9,)),
         ],
         compiler_params=pltpu.CompilerParams(
-            collective_id=0, has_side_effects=True, vmem_limit_bytes=40 << 20
+            collective_id=0, has_side_effects=True, vmem_limit_bytes=50 << 20
         ),
     )(queries, key_rows, value_rows, norm_gain.reshape(1, WIDTH), cotangent)
+    return pl.pallas_call(
+        finish,
+        out_shape=[block] * 4,
+        in_specs=[pl.BlockSpec(memory_space=pltpu.VMEM)] * 7,
+        out_specs=[pl.BlockSpec(memory_space=pltpu.HBM)] * 4,
+        scratch_shapes=[held, held, pltpu.SemaphoreType.DMA((6,))],
+        compiler_params=pltpu.CompilerParams(vmem_limit_bytes=16 << 20),
+    )(*passed)
 
 
 def solution(mesh):

time: 60.4 us -> 51.8 us (0.86)
  local copies, waits for them, and re-layouts: 9.46 us -> 0 us
  Pallas kernels: 50 us -> 51.1 us
    unnamed x14 -> x0, local copies, waits for them, and re-layouts: 9.46 us -> none
    pallas_call x1 -> x2, Pallas kernels: 50 us -> 51.1 us  [the longest x1 48.2 us: per_device(): pl.pallas_call(kernel, out_shape=[held, held, held, held, held32, held32,...]
where the time goes in v2:
time: 51.8 us
  Pallas kernels  51.1 us (99%)
  between operations  0.64 us (1%)
    pallas_call x1, Pallas kernels, per_device(): pl.pallas_call(kernel, out_shape=[held, held, held, held, held32, held32,...  48.2 us
    pallas_call x1, Pallas kernels, per_device(): pl.pallas_call(finish, out_shape=[block] * 4, in_specs=[pl.BlockSpec(memo...  2.94 us

profile of v2, /device:TPU:1, one launch (start us, length us, event | category | flops | bytes accessed | tf_op | source)
XLA Modules:
  0.0 51.8 jit_solution(12624388843973420525)
XLA Ops:
  0.6 48.2 %shard_map.84 = (bf16[512,1024]{1,0:T(8,128)(2,1)S(1)}, bf16[512,1024]{1,0:T(8,128)(2,1)S(1)}, bf16[512,1024]{1,0:T(8,128)(2,1)S(1)}, bf16[512,1024]{1,0:T(8,128...) custom-call(bf16[512,1024]{1,0:T(8,128)(2,1)} %q_hbm.1, ...), custom_call_target="tpu_custom_call" | custom-call | tf_op jit(solution)/shard_map/pallas_call | solution.py:325
  48.8 2.9 %shard_map.85 = (bf16[512,1024]{1,0:T(8,128)(2,1)}, bf16[512,1024]{1,0:T(8,128)(2,1)}, bf16[512,1024]{1,0:T(8,128)(2,1)}, bf16[512,1024]{1,0:T(8,128)(2,1)}) custom-call(bf16[512,1024]{1,0:T(8,128)(2,1)S(1)} %get-tuple-element.11.normed, bf16[512,1024]{1,0:T(8,128)(2,1)S(1)} %get-tuple-element.12.grad_q, bf16[512,1024]{1,0:T(8,128)(2,1)S(1)} %get-tuple-element.13.k, ...), custom_call_target="tpu_custom_call" | custom-call | tf_op jit(solution)/shard_map/pallas_call | solution.py:358

commit v3 on v1

v3 whole, which is shorter than its diff:
```python
import functools

import jax
import jax.numpy as jnp
from jax import lax
from jax.experimental import pallas as pl
from jax.experimental.pallas import tpu as pltpu
from jax.sharding import PartitionSpec as P

MESH = pl.DeviceIdType.MESH
F32 = jnp.float32
BF16 = jnp.bfloat16
DH = 128
TOK = 512
HEADS = 8
WIDTH = HEADS * DH
HALF = HEADS // 2 * DH
NY, NZ, NX = 4, 8, 4
CHIPS = NY * NZ
PIECE = HALF // CHIPS
FULL_WIDTH = WIDTH * NX
CUT = TOK // 2
FAR_REACH = 6
BLOCKS = 2
ROWS = TOK // BLOCKS


def far_first():
    def reach(offset):
        return min(offset[0], NY - offset[0]) + min(offset[1], NZ - offset[1])

    offsets = [(dy, dz) for dy in range(NY) for dz in range(NZ) if dy or dz]
    offsets = sorted(offsets, key=lambda offset: -reach(offset))
    far = [offset for offset in offsets if reach(offset) >= FAR_REACH]
    return far, offsets[len(far) :]


def nn(a, b):
    return lax.dot_general(a, b, (((1,), (0,)), ((), ())), preferred_element_type=F32)


def nt(a, b):
    return lax.dot_general(a, b, (((1,), (1,)), ((), ())), preferred_element_type=F32)


def tn(a, b):
    return lax.dot_general(a, b, (((0,), (0,)), ((), ())), preferred_element_type=F32)


def await_bytes(ref, sem):
    pltpu.make_async_copy(ref, ref, sem).wait()


def kernel(
    q_hbm,
    k_hbm,
    v_hbm,
    gain_hbm,
    c_hbm,
    normed,
    grad_q,
    grad_k,
    grad_v,
    k,
    v,
    part_k,
    part_v,
    suffix,
    q,
    gain,
    c,
    q8,
    q_turned,
    g,
    w,
    att,
    inv_ref,
    fac_ref,
    grad_state,
    state_own,
    state_out,
    state_in,
    chip_sum,
    owned,
    scanned,
    chip_scan,
    scan_out,
    scan,
    far_in,
    far_out,
    far_scan,
    stats,
    load_sem,
    send_sem,
    recv_sem,
):
    place = lax.axis_index("ctx")
    hx = lax.axis_index("head")
    chip = lax.div(place, 2)
    core = lax.rem(place, 2)
    chip_y = lax.div(chip, NZ)
    chip_z = lax.rem(chip, NZ)
    sibling = (chip * 2 + 1 - core, hx)

    def chip_at(dy, dz):
        return lax.rem(chip_y + dy, NY) * NZ + lax.rem(chip_z + dz, NZ)

    far, near = far_first()
    barrier = pltpu.get_barrier_semaphore()

    def greet(device):
        pl.semaphore_signal(barrier, inc=1, device_id=device, device_id_type=MESH)

    for dy, dz in far:
        greet((chip_at(dy, dz) * 2 + core, hx))
        greet((chip_at(dy, dz) * 2 + 1 - core, hx))
    for dy, dz in near:
        greet((chip_at(dy, dz) * 2 + core, hx))
    for step in range(1, NX):
        greet((place, lax.rem(hx + step, NX)))
    greet(sibling)
    greeted = 2 * len(far) + len(near) + NX

    loads = [
        pltpu.make_async_copy(src, dst, load_sem.at[n])
        for n, (src, dst) in enumerate(
            [(k_hbm, k), (v_hbm, v), (q_hbm, q), (gain_hbm, gain), (c_hbm, c)]
        )
    ]
    for load in loads:
        load.start()

    def columns(h):
        return pl.ds(pl.multiple_of(h * DH, DH), DH)

    def rows_of(h):
        return pl.ds(pl.multiple_of(h * DH, DH), DH)

    theirs = pl.multiple_of((1 - core) * HALF, HALF)
    ours = pl.multiple_of(core * HALF, HALF)

    def send(src, dst, n, device):
        pltpu.make_async_remote_copy(
            src_ref=src,
            dst_ref=dst,
            send_sem=send_sem.at[n],
            recv_sem=recv_sem.at[n],
            device_id=device,
            device_id_type=MESH,
        ).start()

    def scan_begin(s, local_state, first):
        def give(i, carry):
            state_out[s, 1 - core, rows_of(i), :] = local_state(
                (1 - core) * (HEADS // 2) + i
            ).astype(BF16)
            return carry

        def keep(i, carry):
            state = local_state(core * (HEADS // 2) + i)
            state_own[s, rows_of(i), :] = state
            state_out[s, core, rows_of(i), :] = state.astype(BF16)
            return carry

        lax.fori_loop(0, HEADS // 2, give, 0, unroll=True)
        if first:
            lax.fori_loop(0, HEADS // 2, keep, 0, unroll=True)
            pl.semaphore_wait(barrier, greeted)
        send(state_out.at[s, 1 - core], state_in.at[s], 6 * s, sibling)
        if not first:
            lax.fori_loop(0, HEADS // 2, keep, 0, unroll=True)
        for j, (dy, dz) in enumerate(far):
            other = chip_at(dy, dz)
            piece = pl.ds(pl.multiple_of(other * PIECE, PIECE), PIECE)
            for half in range(2):
                send(
                    state_out.at[s, half, piece],
                    far_in.at[s, j, core],
                    6 * s + 4,
                    (other * 2 + half, hx),
                )
        await_bytes(state_in.at[s], recv_sem.at[6 * s])
        both = state_own[s] + state_in[s].astype(F32)
        chip_sum[s] = both.astype(BF16).reshape(CHIPS, PIECE, DH)
        for dy, dz in near:
            other = chip_at(dy, dz)
            send(chip_sum.at[s, other], owned.at[s, chip], 6 * s + 1, (other * 2 + core, hx))
        owned[s, chip] = chip_sum[s, chip]
        for dy, dz in far:
            chip_scan[s, chip_at(dy, dz)] = jnp.zeros((PIECE, DH), BF16)

    def scan_middle(s, backward):
        leader = 1 if backward else 0
        await_bytes(far_in.at[s], recv_sem.at[6 * s + 4])
        for j, (dy, dz) in enumerate(far):
            both = far_in[s, j, 0].astype(F32) + far_in[s, j, 1].astype(F32)
            owned[s, chip_at(NY - dy, NZ - dz)] = both.astype(BF16)
        await_bytes(owned.at[s, pl.ds(0, len(near))], recv_sem.at[6 * s + 1])
        total = jnp.zeros((PIECE, DH), F32)
        for n in range(CHIPS):
            one = CHIPS - 1 - n if backward else n
            scanned[s, one] = total.astype(BF16)
            total = total + owned[s, one].astype(F32)
        for j, (dy, dz) in enumerate(far):
            other = chip_at(NY - dy, NZ - dz)
            ahead = scanned[s, other].astype(F32) + far_in[s, j, leader].astype(F32)
            far_out[s, j] = ahead.astype(BF16)
            for half in range(2):
                send(
                    scanned.at[s, other] if half == leader else far_out.at[s, j],
                    far_scan.at[s, j, core],
                    6 * s + 5,
                    (other * 2 + half, hx),
                )
        for dy, dz in near:
            other = chip_at(dy, dz)
            send(scanned.at[s, other], chip_scan.at[s, chip], 6 * s + 2, (other * 2 + core, hx))
        chip_scan[s, chip] = scanned[s, chip]

    def scan_end(s, backward, scale, own_half):
        await_bytes(chip_scan.at[s, pl.ds(0, len(near))], recv_sem.at[6 * s + 2])
        ahead = chip_scan[s].astype(F32).reshape(HALF, DH)
        leads = core == (1 if backward else 0)
        give = ahead + jnp.where(leads, state_own[s], 0.0)
        scan_out[s] = (give * scale).astype(BF16)
        send(scan_out.at[s], scan.at[s, pl.ds(ours, HALF)], 6 * s + 3, sibling)
        keep = ahead + jnp.where(leads, 0.0, state_in[s].astype(F32))
        scan[s, pl.ds(ours, HALF), :] = (keep * scale).astype(BF16)

        def place_far(half, base):
            for j, (dy, dz) in enumerate(far):
                at = pl.multiple_of(base + chip_at(dy, dz) * PIECE, PIECE)
                piece = far_scan[s, j, half].astype(F32) * scale
                scan[s, pl.ds(at, PIECE), :] = piece.astype(BF16)

        await_bytes(far_scan.at[s], recv_sem.at[6 * s + 5])
        place_far(core, ours)
        for i in range(HEADS // 2):
            own_half(i)
        await_bytes(scan_out.at[s], recv_sem.at[6 * s + 3])
        place_far(1 - core, theirs)

    row_at = lax.broadcasted_iota(jnp.int32, (CUT, CUT), 0)
    col_at = lax.broadcasted_iota(jnp.int32, (CUT, CUT), 1)
    causal = col_at <= row_at

    def lower(scores):
        return jnp.where(causal, scores, 0.0).astype(BF16)

    loads[0].wait()
    loads[1].wait()
    scan_begin(0, lambda h: tn(k[:, columns(h)], v[:, columns(h)]), True)
    for load in loads[2:]:
        load.wait()

    def inside(h, carry):
        col = columns(h)
        q8_h = q[:, col] * jnp.asarray(1.0 / DH, BF16)
        q8[:, col] = q8_h
        q_turned[rows_of(h), :] = q[:, col].T
        k_h, v_h = k[:, col], v[:, col]
        w00 = lower(nt(q8_h[:CUT], k_h[:CUT]))
        w[h, :CUT, :CUT] = w00
        att[:CUT, col] = nn(w00, v_h[:CUT])
        w10 = nt(q8_h[CUT:], k_h[:CUT]).astype(BF16)
        w11 = lower(nt(q8_h[CUT:], k_h[CUT:]))
        w[h, CUT:, :CUT] = w10
        w[h, CUT:, CUT:] = w11
        att[CUT:, col] = nn(w10, v_h[:CUT]) + nn(w11, v_h[CUT:])
        return carry

    lax.fori_loop(0, HEADS // 2, inside, 0)
    scan_middle(0, False)
    lax.fori_loop(HEADS // 2, HEADS, inside, 0)

    def across(rows, h):
        col = columns(h)
        att[rows, col] += nn(q8[rows, col], scan[0, rows_of(h), :])

    scan_end(0, False, 1.0, lambda i: across(slice(0, TOK), core * (HEADS // 2) + i))

    for b in range(BLOCKS):
        rows = slice(b * ROWS, (b + 1) * ROWS)
        for i in range(HEADS // 2):
            across(rows, (1 - core) * (HEADS // 2) + i)

        def row_sums(i, carry):
            at = pl.ds(pl.multiple_of(b * ROWS + i * DH, DH), DH)
            squares = jnp.zeros((DH, DH), F32)
            inner = jnp.zeros((DH, DH), F32)
            for h in range(HEADS):
                col = slice(h * DH, (h + 1) * DH)
                a = att[at, col]
                squares += a * a
                inner += a * (gain[:, col] * c[at, col].astype(F32))
            to = pl.ds(pl.multiple_of(i * DH, DH), DH)
            stats[b, hx, 0:1, to] = jnp.sum(squares.T, axis=0, keepdims=True)
            stats[b, hx, 1:2, to] = jnp.sum(inner.T, axis=0, keepdims=True)
            return carry

        lax.fori_loop(0, ROWS // DH, row_sums, 0, unroll=True)
        for step in range(1, NX):
            send(stats.at[b, hx], stats.at[b, hx], 12 + b, (place, lax.rem(hx + step, NX)))

    def gradient(b, h):
        rows = slice(b * ROWS, (b + 1) * ROWS)
        col = columns(h)
        scaled = gain[:, col] * c[rows, col].astype(F32)
        g_h = ((scaled - att[rows, col] * fac_ref[rows, :]) * inv_ref[rows, :]).astype(BF16)
        g[rows, col] = g_h
        return nn(q_turned[rows_of(h), rows], g_h)

    for b in range(BLOCKS):
        await_bytes(stats.at[b, pl.ds(0, NX - 1)], recv_sem.at[12 + b])
        sums = stats[b, 0] + stats[b, 1] + stats[b, 2] + stats[b, 3]
        mean_square = sums[0:1] * (1.0 / FULL_WIDTH) + 1e-6
        inverse = 1.0 / jnp.sqrt(mean_square)
        factor = sums[1:2] / (FULL_WIDTH * mean_square)
        for i in range(ROWS // DH):
            some = slice(i * DH, (i + 1) * DH)
            rows = slice(b * ROWS + i * DH, b * ROWS + (i + 1) * DH)
            inv_ref[rows, :] = jnp.broadcast_to(inverse[:, some], (DH, DH)).T
            fac_ref[rows, :] = jnp.broadcast_to(factor[:, some], (DH, DH)).T
        if b < BLOCKS - 1:
            for h in range(HEADS):
                state = gradient(b, h)
                grad_state[rows_of(h), :] = state if b == 0 else grad_state[rows_of(h), :] + state

    def gradient_state(h):
        return grad_state[rows_of(h), :] + gradient(BLOCKS - 1, h)

    scan_begin(1, gradient_state, False)

    def inside_back(h, carry):
        col = columns(h)
        normed[:, col] = (gain[:, col] * att[:, col] * inv_ref[...]).astype(BF16)
        q_h, k_h, v_h, g_h = q[:, col], k[:, col], v[:, col], g[:, col]
        g8 = g_h * jnp.asarray(1.0 / DH, BF16)
        before = scan[0, rows_of(h), :]
        u00 = lower(nt(g8[:CUT], v_h[:CUT]))
        u10 = nt(g8[CUT:], v_h[:CUT]).astype(BF16)
        u11 = lower(nt(g8[CUT:], v_h[CUT:]))
        grad_q[:CUT, col] = (nn(u00, k_h[:CUT]) + nt(g8[:CUT], before)).astype(BF16)
        grad_q[CUT:, col] = (
            nn(u10, k_h[:CUT]) + nn(u11, k_h[CUT:]) + nt(g8[CUT:], before)
        ).astype(BF16)
        part_k[:CUT, col] = tn(u00, q_h[:CUT]) + tn(u10, q_h[CUT:])
        part_k[CUT:, col] = tn(u11, q_h[CUT:])
        part_v[:CUT, col] = tn(w[h, :CUT, :CUT], g_h[:CUT]) + tn(w[h, CUT:, :CUT], g_h[CUT:])
        part_v[CUT:, col] = tn(w[h, CUT:, CUT:], g_h[CUT:])
        return carry

    lax.fori_loop(0, HEADS // 2, inside_back, 0)
    scan_middle(1, True)
    lax.fori_loop(HEADS // 2, HEADS, inside_back, 0)

    def finish_own(i):
        h = core * (HEADS // 2) + i
        col = columns(h)
        after = scan[1, rows_of(h), :]
        to = slice(i * DH, (i + 1) * DH)
        grad_k[:, to] = (part_k[:, col] + nt(v[:, col], after)).astype(BF16)
        grad_v[:, to] = (part_v[:, col] + nn(k[:, col], after)).astype(BF16)

    scan_end(1, True, 1.0 / DH, finish_own)

    suffix[...] = scan[1, pl.ds(theirs, HALF), :]

    for s in range(2):
        await_bytes(state_in.at[s], send_sem.at[6 * s])
        await_bytes(chip_sum.at[s, pl.ds(0, len(near))], send_sem.at[6 * s + 1])
        await_bytes(scanned.at[s, pl.ds(0, len(near))], send_sem.at[6 * s + 2])
        await_bytes(scan_out.at[s], send_sem.at[6 * s + 3])
        await_bytes(far_in.at[s], send_sem.at[6 * s + 4])
        await_bytes(far_scan.at[s], send_sem.at[6 * s + 5])
    for b in range(BLOCKS):
        await_bytes(stats.at[b, pl.ds(0, NX - 1)], send_sem.at[12 + b])


def finish(normed, grad_q, grad_k, grad_v, k, v, part_k, part_v, suffix, *rest):
    normed_out, grad_q_out, grad_k_out, grad_v_out, last_k, last_v, sem = rest
    core = lax.rem(lax.axis_index("ctx"), 2)
    ours = pl.ds(pl.multiple_of(core * HALF, HALF), HALF)
    stores = []

    def store(src, dst):
        copy = pltpu.make_async_copy(src, dst, sem.at[len(stores)])
        copy.start()
        stores.append(copy)

    store(normed, normed_out)
    store(grad_q, grad_q_out)
    store(grad_k, grad_k_out.at[:, ours])
    store(grad_v, grad_v_out.at[:, ours])
    for i in range(HEADS // 2):
        to = slice(i * DH, (i + 1) * DH)
        col = pl.ds(pl.multiple_of((1 - core) * HALF + i * DH, DH), DH)
        after = suffix[to, :]
        last_k[:, to] = (part_k[:, col] + nt(v[:, col], after)).astype(BF16)
        last_v[:, to] = (part_v[:, col] + nn(k[:, col], after)).astype(BF16)
        if i % 2:
            pair = pl.ds((i - 1) * DH, 2 * DH)
            out = pl.ds(pl.multiple_of((1 - core) * HALF + (i - 1) * DH, 2 * DH), 2 * DH)
            store(last_k.at[:, pair], grad_k_out.at[:, out])
            store(last_v.at[:, pair], grad_v_out.at[:, out])
    for copy in stores:
        copy.wait()


def per_device(queries, key_rows, value_rows, norm_gain, cotangent):
    block = jax.ShapeDtypeStruct((TOK, WIDTH), BF16)
    held = pltpu.VMEM((TOK, WIDTH), BF16)
    held32 = pltpu.VMEM((TOK, WIDTH), F32)
    held_half = pltpu.VMEM((TOK, HALF), BF16)
    suffix = pltpu.VMEM((HALF, DH), BF16)
    half = pltpu.VMEM((2, HALF, DH), BF16)
    pieces = pltpu.VMEM((2, CHIPS, PIECE, DH), BF16)
    far = len(far_first()[0])
    passed = pl.pallas_call(
        kernel,
        out_shape=[held, held, held_half, held_half, held, held, held32, held32, suffix],
        in_specs=[pl.BlockSpec(memory_space=pltpu.HBM)] * 5,
        out_specs=[pl.BlockSpec(memory_space=pltpu.VMEM)] * 9,
        scratch_shapes=[
            held,
            pltpu.VMEM((1, WIDTH), F32),
            held,
            held,
            pltpu.VMEM((WIDTH, TOK), BF16),
            held,
            pltpu.VMEM((HEADS, TOK, TOK), BF16),
            held32,
            pltpu.VMEM((TOK, DH), F32),
            pltpu.VMEM((TOK, DH), F32),
            pltpu.VMEM((WIDTH, DH), F32),
            pltpu.VMEM((2, HALF, DH), F32),
            pltpu.VMEM((2, 2, HALF, DH), BF16),
            half,
            pieces,
            pieces,
            pieces,
            pieces,
            half,
            pltpu.VMEM((2, 2 * HALF, DH), BF16),
            pltpu.VMEM((2, far, 2, PIECE, DH), BF16),
            pltpu.VMEM((2, far, PIECE, DH), BF16),
            pltpu.VMEM((2, far, 2, PIECE, DH), BF16),
            pltpu.VMEM((BLOCKS, NX, 2, ROWS), F32),
            pltpu.SemaphoreType.DMA((5,)),
            pltpu.SemaphoreType.DMA((12 + BLOCKS,)),
            pltpu.SemaphoreType.DMA((12 + BLOCKS,)),
        ],
        compiler_params=pltpu.CompilerParams(
            collective_id=0, has_side_effects=True, vmem_limit_bytes=50 << 20
        ),
    )(queries, key_rows, value_rows, norm_gain.reshape(1, WIDTH), cotangent)
    return pl.pallas_call(
        finish,
        out_shape=[block] * 4,
        in_specs=[pl.BlockSpec(memory_space=pltpu.VMEM)] * 9,
        out_specs=[pl.BlockSpec(memory_space=pltpu.HBM)] * 4,
        scratch_shapes=[held_half, held_half, pltpu.SemaphoreType.DMA((4 + HEADS // 2,))],
        compiler_params=pltpu.CompilerParams(vmem_limit_bytes=16 << 20),
    )(*passed)


def solution(mesh):
    placed = (P("ctx", "head"), P("ctx", "head"), P("ctx", "head"), P("head"), P("ctx", "head"))
    return jax.shard_map(
        per_device,
        mesh=mesh,
        in_specs=placed,
        out_specs=(P("ctx", "head"), P("ctx", "head"), P("ctx", "head"), P("ctx", "head")),
        check_vma=False,
    )
```

time: 60.4 us -> 49.5 us (0.82)
  local copies, waits for them, and re-layouts: 9.46 us -> 0 us
  Pallas kernels: 50 us -> 48.8 us
    unnamed x14 -> x0, local copies, waits for them, and re-layouts: 9.46 us -> none
    pallas_call x1 -> x2, Pallas kernels: 50 us -> 48.8 us  [the longest x1 46.7 us: per_device(): pl.pallas_call(kernel, out_shape=[held, held, held_half, held_half, held,...]
where the time goes in v3:
time: 49.5 us; the launch traced here: 49.4 us
  Pallas kernels  48.8 us (99%)
  between operations  0.64 us (1%)
    pallas_call x1, Pallas kernels, per_device(): pl.pallas_call(kernel, out_shape=[held, held, held_half, held_half, held,...  46.7 us
    pallas_call x1, Pallas kernels, per_device(): pl.pallas_call(finish, out_shape=[block] * 4, in_specs=[pl.BlockSpec(memo...  2.07 us

profile of v3, /device:TPU:1, one launch (start us, length us, event | category | flops | bytes accessed | tf_op | source)
XLA Modules:
  0.0 49.4 jit_solution(757263556556463744)
XLA Ops:
  0.6 46.7 %shard_map.84 = (bf16[512,1024]{1,0:T(8,128)(2,1)S(1)}, bf16[512,1024]{1,0:T(8,128)(2,1)S(1)}, bf16[512,512]{1,0:T(8,128)(2,1)S(1)}, bf16[512,512]{1,0:T(8,128)(...) custom-call(bf16[512,1024]{1,0:T(8,128)(2,1)} %q_hbm.1, ...), custom_call_target="tpu_custom_call" | custom-call | tf_op jit(solution)/shard_map/pallas_call | solution.py:419
  47.3 2.1 %shard_map.85 = (bf16[512,1024]{1,0:T(8,128)(2,1)}, bf16[512,1024]{1,0:T(8,128)(2,1)}, bf16[512,1024]{1,0:T(8,128)(2,1)}, bf16[512,1024]{1,0:T(8,128)(2,1)}) custom-call(bf16[512,1024]{1,0:T(8,128)(2,1)S(1)} %get-tuple-element.13.normed, bf16[512,1024]{1,0:T(8,128)(2,1)S(1)} %get-tuple-element.14.grad_q, bf16[512,512]{1,0:T(8,128)(2,1)S(1)} %get-tuple-element.15.grad_k, ...), custom_call_target="tpu_custom_call" | custom-call | tf_op jit(solution)/shard_map/pallas_call | solution.py:457

commit v4 on v1

v4 whole, which is shorter than its diff:
```python
import functools

import jax
import jax.numpy as jnp
from jax import lax
from jax.experimental import pallas as pl
from jax.experimental.pallas import tpu as pltpu
from jax.sharding import PartitionSpec as P

MESH = pl.DeviceIdType.MESH
F32 = jnp.float32
BF16 = jnp.bfloat16
DH = 128
TOK = 512
HEADS = 8
WIDTH = HEADS * DH
HALF = HEADS // 2 * DH
NY, NZ, NX = 4, 8, 4
CHIPS = NY * NZ
PIECE = HALF // CHIPS
FULL_WIDTH = WIDTH * NX
CUT = TOK // 2


def far_first():
    def reach(offset):
        return min(offset[0], NY - offset[0]) + min(offset[1], NZ - offset[1])

    offsets = [(dy, dz) for dy in range(NY) for dz in range(NZ) if dy or dz]
    return sorted(offsets, key=lambda offset: -reach(offset))


def nn(a, b):
    return lax.dot_general(a, b, (((1,), (0,)), ((), ())), preferred_element_type=F32)


def nt(a, b):
    return lax.dot_general(a, b, (((1,), (1,)), ((), ())), preferred_element_type=F32)


def tn(a, b):
    return lax.dot_general(a, b, (((0,), (0,)), ((), ())), preferred_element_type=F32)


def await_bytes(ref, sem):
    pltpu.make_async_copy(ref, ref, sem).wait()


def kernel(
    q_hbm,
    k_hbm,
    v_hbm,
    gain_hbm,
    c_hbm,
    normed,
    grad_q,
    grad_k,
    grad_v,
    k,
    v,
    part_k,
    part_v,
    suffix,
    q,
    kx,
    vx,
    c,
    gain,
    q8,
    q_turned,
    g,
    w,
    att,
    inv_ref,
    fac_ref,
    normed_out,
    grad_q_out,
    part_k_out,
    part_v_out,
    state_own,
    state_out,
    state_in,
    grad_state,
    chip_sum,
    owned,
    scanned,
    chip_scan,
    suffix_out,
    scan,
    stats,
    load_sem,
    send_sem,
    recv_sem,
):
    place = lax.axis_index("ctx")
    hx = lax.axis_index("head")
    chip = lax.div(place, 2)
    core = lax.rem(place, 2)
    chip_y = lax.div(chip, NZ)
    chip_z = lax.rem(chip, NZ)
    twin = chip * 2 + 1 - core
    sibling = (twin, hx)

    def chip_at(dy, dz):
        return lax.rem(chip_y + dy, NY) * NZ + lax.rem(chip_z + dz, NZ)

    offsets = far_first()
    barrier = pltpu.get_barrier_semaphore()

    def greet(device):
        pl.semaphore_signal(barrier, inc=1, device_id=device, device_id_type=MESH)

    for dy, dz in offsets:
        greet((chip_at(dy, dz) * 2 + core, hx))
    row = []
    for step in range(1, NX):
        row += [(place, lax.rem(hx + step, NX)), (twin, lax.rem(hx + step, NX))]
    row.append(sibling)
    for device in row:
        greet(device)

    ours = pl.ds(pl.multiple_of(core * HALF, HALF), HALF)
    theirs = pl.ds(pl.multiple_of((1 - core) * HALF, HALF), HALF)
    loads = [
        pltpu.make_async_copy(src, dst, load_sem.at[n])
        for n, (src, dst) in enumerate(
            [
                (k_hbm, k),
                (v_hbm, v),
                (q_hbm.at[:, ours], q.at[:, ours]),
                (k_hbm.at[:, ours], kx.at[:, ours]),
                (v_hbm.at[:, ours], vx.at[:, ours]),
                (c_hbm.at[:, ours], c.at[:, ours]),
                (gain_hbm.at[:, ours], gain.at[:, pl.ds(0, HALF)]),
                (gain_hbm.at[:, ours], gain.at[:, pl.ds(HALF, HALF)]),
            ]
        )
    ]
    for load in loads:
        load.start()

    def columns(h):
        return pl.ds(pl.multiple_of(h * DH, DH), DH)

    def send(src, dst, n, device):
        pltpu.make_async_remote_copy(
            src_ref=src,
            dst_ref=dst,
            send_sem=send_sem.at[n],
            recv_sem=recv_sem.at[n],
            device_id=device,
            device_id_type=MESH,
        ).start()

    def scan_begin(s, both):
        chip_sum[s] = both.astype(BF16).reshape(CHIPS, PIECE, DH)
        for dy, dz in offsets:
            other = chip_at(dy, dz)
            send(chip_sum.at[s, other], owned.at[s, chip], 2 * s, (other * 2 + core, hx))
        owned[s, chip] = chip_sum[s, chip]

    def scan_middle(s, backward):
        await_bytes(owned.at[s, pl.ds(0, CHIPS - 1)], recv_sem.at[2 * s])
        total = jnp.zeros((PIECE, DH), F32)
        for n in range(CHIPS):
            one = CHIPS - 1 - n if backward else n
            scanned[s, one] = total.astype(BF16)
            total = total + owned[s, one].astype(F32)
        for dy, dz in offsets:
            other = chip_at(dy, dz)
            send(scanned.at[s, other], chip_scan.at[s, chip], 2 * s + 1, (other * 2 + core, hx))
        chip_scan[s, chip] = scanned[s, chip]

    def scan_end(s):
        await_bytes(chip_scan.at[s, pl.ds(0, CHIPS - 1)], recv_sem.at[2 * s + 1])
        return chip_scan[s].astype(F32).reshape(HALF, DH)

    row_at = lax.broadcasted_iota(jnp.int32, (CUT, CUT), 0)
    col_at = lax.broadcasted_iota(jnp.int32, (CUT, CUT), 1)
    causal = col_at <= row_at

    def lower(scores):
        return jnp.where(causal, scores, 0.0).astype(BF16)

    loads[0].wait()
    loads[1].wait()
    for i in range(HEADS // 2):
        col = columns((1 - core) * (HEADS // 2) + i)
        state_out[columns(i), :] = tn(k[:, col], v[:, col]).astype(BF16)
    for i in range(HEADS // 2):
        col = columns(core * (HEADS // 2) + i)
        state_own[columns(i), :] = tn(k[:, col], v[:, col])
    pl.semaphore_wait(barrier, len(offsets) + len(row))
    send(state_out, state_in, 4, sibling)
    await_bytes(state_in, recv_sem.at[4])
    scan_begin(0, state_own[...] + state_in[...].astype(F32))
    shared = [(q_hbm, q), (k_hbm, kx), (v_hbm, vx), (c_hbm, c)]
    for n, (src, dst) in enumerate(shared):
        send(src.at[:, theirs], dst.at[:, ours], 8 + n, sibling)
    for load in loads[2:]:
        load.wait()

    def inside(h, carry):
        col = columns(h)
        q8_h = q[:, col] * jnp.asarray(1.0 / DH, BF16)
        q8[:, col] = q8_h
        q_turned[col, :] = q[:, col].T
        k_h, v_h = kx[:, col], vx[:, col]
        w00 = lower(nt(q8_h[:CUT], k_h[:CUT]))
        w[h, :CUT, :CUT] = w00
        att[:CUT, col] = nn(w00, v_h[:CUT])
        w10 = nt(q8_h[CUT:], k_h[:CUT]).astype(BF16)
        w11 = lower(nt(q8_h[CUT:], k_h[CUT:]))
        w[h, CUT:, :CUT] = w10
        w[h, CUT:, CUT:] = w11
        att[CUT:, col] = nn(w10, v_h[:CUT]) + nn(w11, v_h[CUT:])
        return carry

    first_own = core * (HEADS // 2)
    first_other = (1 - core) * (HEADS // 2)
    lax.fori_loop(first_own, first_own + HEADS // 2, inside, 0)
    scan_middle(0, False)
    for n, (src, dst) in enumerate(shared):
        await_bytes(dst.at[:, theirs], recv_sem.at[8 + n])
    lax.fori_loop(first_other, first_other + HEADS // 2, inside, 0)
    ahead = scan_end(0)
    scan[0, :HALF, :] = ahead.astype(BF16)
    between = jnp.where(core == 0, state_own[...], state_in[...].astype(F32))
    scan[0, HALF:, :] = (ahead + between).astype(BF16)

    slot = hx * 2 + core
    for b in range(2):
        for h in range(b * HEADS // 2, (b + 1) * HEADS // 2):
            col = slice(h * DH, (h + 1) * DH)
            att[:, col] += nn(q8[:, col], scan[0, col, :])
        for i in range(TOK // DH):
            rows = slice(i * DH, (i + 1) * DH)
            squares = jnp.zeros((DH, DH), F32)
            inner = jnp.zeros((DH, DH), F32)
            for h in range(b * HEADS // 2, (b + 1) * HEADS // 2):
                col = slice(h * DH, (h + 1) * DH)
                a = att[rows, col]
                squares += a * a
                inner += a * (gain[:, col] * c[rows, col].astype(F32))
            stats[b, slot, 0:1, rows] = jnp.sum(squares.T, axis=0, keepdims=True)
            stats[b, slot, 1:2, rows] = jnp.sum(inner.T, axis=0, keepdims=True)
        for device in row:
            send(stats.at[b, slot], stats.at[b, slot], 6 + b, device)

    for b in range(2):
        await_bytes(stats.at[b, pl.ds(0, len(row))], recv_sem.at[6 + b])
        sums = stats[b, 0]
        for n in range(1, len(row) + 1):
            sums = sums + stats[b, n]
        mean_square = sums[0:1] * (1.0 / FULL_WIDTH) + 1e-6
        inverse = 1.0 / jnp.sqrt(mean_square)
        factor = sums[1:2] / (FULL_WIDTH * mean_square)
        for i in range(TOK // DH):
            rows = slice(i * DH, (i + 1) * DH)
            inv_ref[b, rows, :] = jnp.broadcast_to(inverse[:, rows], (DH, DH)).T
            fac_ref[b, rows, :] = jnp.broadcast_to(factor[:, rows], (DH, DH)).T
        for h in range(b * HEADS // 2, (b + 1) * HEADS // 2):
            col = slice(h * DH, (h + 1) * DH)
            scaled = gain[:, col] * c[:, col].astype(F32)
            g_h = ((scaled - att[:, col] * fac_ref[b]) * inv_ref[b]).astype(BF16)
            g[:, col] = g_h
            grad_state[col, :] = nn(q_turned[col, :], g_h)
    scan_begin(1, grad_state[:HALF, :] + grad_state[HALF:, :])

    def inside_back(block, i, to_normed, to_q, to_k, to_v, to):
        h = block * (HEADS // 2) + i
        col = columns(h)
        inverse = inv_ref[block]
        to_normed[:, to] = (gain[:, col] * att[:, col] * inverse).astype(BF16)
        q_h, k_h, v_h, g_h = q[:, col], kx[:, col], vx[:, col], g[:, col]
        g8 = g_h * jnp.asarray(1.0 / DH, BF16)
        before = scan[0, col, :]
        u00 = lower(nt(g8[:CUT], v_h[:CUT]))
        u10 = nt(g8[CUT:], v_h[:CUT]).astype(BF16)
        u11 = lower(nt(g8[CUT:], v_h[CUT:]))
        to_q[:CUT, to] = (nn(u00, k_h[:CUT]) + nt(g8[:CUT], before)).astype(BF16)
        to_q[CUT:, to] = (
            nn(u10, k_h[:CUT]) + nn(u11, k_h[CUT:]) + nt(g8[CUT:], before)
        ).astype(BF16)
        to_k[:CUT, to] = tn(u00, q_h[:CUT]) + tn(u10, q_h[CUT:])
        to_k[CUT:, to] = tn(u11, q_h[CUT:])
        to_v[:CUT, to] = tn(w[h, :CUT, :CUT], g_h[:CUT]) + tn(w[h, CUT:, :CUT], g_h[CUT:])
        to_v[CUT:, to] = tn(w[h, CUT:, CUT:], g_h[CUT:])

    def for_sibling(i, carry):
        inside_back(1 - core, i, normed_out, grad_q_out, part_k_out, part_v_out, columns(i))
        return carry

    def for_own(i, carry):
        inside_back(core, i, normed, grad_q, part_k, part_v, columns(first_own + i))
        return carry

    lax.fori_loop(0, HEADS // 2, for_sibling, 0)
    send(normed_out, normed.at[:, ours], 12, sibling)
    send(grad_q_out, grad_q.at[:, ours], 13, sibling)
    scan_middle(1, True)
    send(part_k_out, part_k.at[:, ours], 14, sibling)
    send(part_v_out, part_v.at[:, ours], 15, sibling)
    lax.fori_loop(0, HEADS // 2, for_own, 0)
    ahead = scan_end(1)
    behind = ahead + grad_state[HALF:, :]
    suffix_out[...] = (jnp.where(core == 0, ahead, behind) * (1.0 / DH)).astype(BF16)
    send(suffix_out, suffix, 5, sibling)
    scan[1, :HALF, :] = (jnp.where(core == 0, behind, ahead) * (1.0 / DH)).astype(BF16)
    for i in range(HEADS // 2):
        col = columns(first_own + i)
        to = slice(i * DH, (i + 1) * DH)
        after = scan[1, to, :]
        grad_k[:, to] = (part_k[:, col] + nt(v[:, col], after)).astype(BF16)
        grad_v[:, to] = (part_v[:, col] + nn(k[:, col], after)).astype(BF16)

    staged = [(normed_out, normed), (grad_q_out, grad_q), (part_k_out, part_k), (part_v_out, part_v)]
    for n, (src, dst) in enumerate(staged):
        await_bytes(dst.at[:, theirs], recv_sem.at[12 + n])
        await_bytes(src, send_sem.at[12 + n])
    for s in range(2):
        await_bytes(chip_sum.at[s, pl.ds(0, CHIPS - 1)], send_sem.at[2 * s])
        await_bytes(scanned.at[s, pl.ds(0, CHIPS - 1)], send_sem.at[2 * s + 1])
    await_bytes(state_out, send_sem.at[4])
    for b in range(2):
        await_bytes(stats.at[b, pl.ds(0, len(row))], send_sem.at[6 + b])
    for n, (src, dst) in enumerate(shared):
        await_bytes(dst.at[:, theirs], send_sem.at[8 + n])
    await_bytes(suffix, recv_sem.at[5])
    await_bytes(suffix_out, send_sem.at[5])


def finish(normed, grad_q, grad_k, grad_v, k, v, part_k, part_v, suffix, *rest):
    normed_out, grad_q_out, grad_k_out, grad_v_out, last_k, last_v, sem = rest
    core = lax.rem(lax.axis_index("ctx"), 2)
    ours = pl.ds(pl.multiple_of(core * HALF, HALF), HALF)
    stores = []

    def store(src, dst):
        copy = pltpu.make_async_copy(src, dst, sem.at[len(stores)])
        copy.start()
        stores.append(copy)

    store(normed, normed_out)
    store(grad_q, grad_q_out)
    store(grad_k, grad_k_out.at[:, ours])
    store(grad_v, grad_v_out.at[:, ours])
    for i in range(HEADS // 2):
        to = slice(i * DH, (i + 1) * DH)
        col = pl.ds(pl.multiple_of((1 - core) * HALF + i * DH, DH), DH)
        after = suffix[to, :]
        last_k[:, to] = (part_k[:, col] + nt(v[:, col], after)).astype(BF16)
        last_v[:, to] = (part_v[:, col] + nn(k[:, col], after)).astype(BF16)
        if i % 2:
            pair = pl.ds((i - 1) * DH, 2 * DH)
            out = pl.ds(pl.multiple_of((1 - core) * HALF + (i - 1) * DH, 2 * DH), 2 * DH)
            store(last_k.at[:, pair], grad_k_out.at[:, out])
            store(last_v.at[:, pair], grad_v_out.at[:, out])
    for copy in stores:
        copy.wait()


def per_device(queries, key_rows, value_rows, norm_gain, cotangent):
    block = jax.ShapeDtypeStruct((TOK, WIDTH), BF16)
    held = pltpu.VMEM((TOK, WIDTH), BF16)
    held32 = pltpu.VMEM((TOK, WIDTH), F32)
    held_half = pltpu.VMEM((TOK, HALF), BF16)
    suffix = pltpu.VMEM((HALF, DH), BF16)
    pieces = pltpu.VMEM((2, CHIPS, PIECE, DH), BF16)
    passed = pl.pallas_call(
        kernel,
        out_shape=[held, held, held_half, held_half, held, held, held32, held32, suffix],
        in_specs=[pl.BlockSpec(memory_space=pltpu.HBM)] * 5,
        out_specs=[pl.BlockSpec(memory_space=pltpu.VMEM)] * 9,
        scratch_shapes=[
            held,
            held,
            held,
            held,
            pltpu.VMEM((1, WIDTH), F32),
            held,
            pltpu.VMEM((WIDTH, TOK), BF16),
            held,
            pltpu.VMEM((HEADS, TOK, TOK), BF16),
            held32,
            pltpu.VMEM((2, TOK, DH), F32),
            pltpu.VMEM((2, TOK, DH), F32),
            held_half,
            held_half,
            pltpu.VMEM((TOK, HALF), F32),
            pltpu.VMEM((TOK, HALF), F32),
            pltpu.VMEM((HALF, DH), F32),
            suffix,
            suffix,
            pltpu.VMEM((WIDTH, DH), F32),
            pieces,
            pieces,
            pieces,
            pieces,
            suffix,
            pltpu.VMEM((2, WIDTH, DH), BF16),
            pltpu.VMEM((2, 2 * NX, 2, TOK), F32),
            pltpu.SemaphoreType.DMA((8,)),
            pltpu.SemaphoreType.DMA((16,)),
            pltpu.SemaphoreType.DMA((16,)),
        ],
        compiler_params=pltpu.CompilerParams(
            collective_id=0, has_side_effects=True, vmem_limit_bytes=50 << 20
        ),
    )(queries, key_rows, value_rows, norm_gain.reshape(1, WIDTH), cotangent)
    return pl.pallas_call(
        finish,
        out_shape=[block] * 4,
        in_specs=[pl.BlockSpec(memory_space=pltpu.VMEM)] * 9,
        out_specs=[pl.BlockSpec(memory_space=pltpu.HBM)] * 4,
        scratch_shapes=[held_half, held_half, pltpu.SemaphoreType.DMA((4 + HEADS // 2,))],
        compiler_params=pltpu.CompilerParams(vmem_limit_bytes=16 << 20),
    )(*passed)


def solution(mesh):
    placed = (P("ctx", "head"), P("ctx", "head"), P("ctx", "head"), P("head"), P("ctx", "head"))
    return jax.shard_map(
        per_device,
        mesh=mesh,
        in_specs=placed,
        out_specs=(P("ctx", "head"), P("ctx", "head"), P("ctx", "head"), P("ctx", "head")),
        check_vma=False,
    )
```

time: 60.4 us -> 48 us (0.79)
  local copies, waits for them, and re-layouts: 9.46 us -> 0 us
  Pallas kernels: 50 us -> 47.3 us
    unnamed x14 -> x0, local copies, waits for them, and re-layouts: 9.46 us -> none
    pallas_call x1 -> x2, Pallas kernels: 50 us -> 47.3 us  [the longest x1 45.2 us: per_device(): pl.pallas_call(kernel, out_shape=[held, held, held_half, held_half, held,...]
where the time goes in v4:
time: 48 us; the launch traced here: 47.9 us
  Pallas kernels  47.3 us (99%)
  between operations  0.64 us (1%)
    pallas_call x1, Pallas kernels, per_device(): pl.pallas_call(kernel, out_shape=[held, held, held_half, held_half, held,...  45.2 us
    pallas_call x1, Pallas kernels, per_device(): pl.pallas_call(finish, out_shape=[block] * 4, in_specs=[pl.BlockSpec(memo...  2.07 us

profile of v4, /device:TPU:1, one launch (start us, length us, event | category | flops | bytes accessed | tf_op | source)
XLA Modules:
  0.0 47.9 jit_solution(9547955807114609325)
XLA Ops:
  0.6 45.2 %shard_map.84 = (bf16[512,1024]{1,0:T(8,128)(2,1)S(1)}, bf16[512,1024]{1,0:T(8,128)(2,1)S(1)}, bf16[512,512]{1,0:T(8,128)(2,1)S(1)}, bf16[512,512]{1,0:T(8,128)(...) custom-call(bf16[512,1024]{1,0:T(8,128)(2,1)} %q_hbm.1, ...), custom_call_target="tpu_custom_call" | custom-call | tf_op jit(solution)/shard_map/pallas_call | solution.py:370
  45.9 2.1 %shard_map.85 = (bf16[512,1024]{1,0:T(8,128)(2,1)}, bf16[512,1024]{1,0:T(8,128)(2,1)}, bf16[512,1024]{1,0:T(8,128)(2,1)}, bf16[512,1024]{1,0:T(8,128)(2,1)}) custom-call(bf16[512,1024]{1,0:T(8,128)(2,1)S(1)} %get-tuple-element.13.normed, bf16[512,1024]{1,0:T(8,128)(2,1)S(1)} %get-tuple-element.14.grad_q, bf16[512,512]{1,0:T(8,128)(2,1)S(1)} %get-tuple-element.15.grad_k, ...), custom_call_target="tpu_custom_call" | custom-call | tf_op jit(solution)/shard_map/pallas_call | solution.py:411

commit v5 on v4

--- a/solution.py
+++ b/solution.py
@@ -99,10 +99,12 @@
     chip_y = lax.div(chip, NZ)
     chip_z = lax.rem(chip, NZ)
     twin = chip * 2 + 1 - core
+    sign = 1 - 2 * core
     sibling = (twin, hx)
 
     def chip_at(dy, dz):
-        return lax.rem(chip_y + dy, NY) * NZ + lax.rem(chip_z + dz, NZ)
+        y = lax.rem(chip_y + NY + sign * dy, NY)
+        return y * NZ + lax.rem(chip_z + NZ + sign * dz, NZ)
 
     offsets = far_first()
     barrier = pltpu.get_barrier_semaphore()
@@ -113,8 +115,8 @@
     for dy, dz in offsets:
         greet((chip_at(dy, dz) * 2 + core, hx))
     row = []
-    for step in range(1, NX):
-        row += [(place, lax.rem(hx + step, NX)), (twin, lax.rem(hx + step, NX))]
+    for step in (2, 1, 3):
+        row += [(twin, lax.rem(hx + step, NX)), (place, lax.rem(hx + step, NX))]
     row.append(sibling)
     for device in row:
         greet(device)
@@ -125,8 +127,10 @@
         pltpu.make_async_copy(src, dst, load_sem.at[n])
         for n, (src, dst) in enumerate(
             [
-                (k_hbm, k),
-                (v_hbm, v),
+                (k_hbm.at[:, theirs], k.at[:, theirs]),
+                (v_hbm.at[:, theirs], v.at[:, theirs]),
+                (k_hbm.at[:, ours], k.at[:, ours]),
+                (v_hbm.at[:, ours], v.at[:, ours]),
                 (q_hbm.at[:, ours], q.at[:, ours]),
                 (k_hbm.at[:, ours], kx.at[:, ours]),
                 (v_hbm.at[:, ours], vx.at[:, ours]),
@@ -136,7 +140,7 @@
             ]
         )
     ]
-    for load in loads:
+    for load in loads[:4]:
         load.start()
 
     def columns(h):
@@ -187,6 +191,10 @@
     for i in range(HEADS // 2):
         col = columns((1 - core) * (HEADS // 2) + i)
         state_out[columns(i), :] = tn(k[:, col], v[:, col]).astype(BF16)
+    loads[2].wait()
+    loads[3].wait()
+    for load in loads[4:]:
+        load.start()
     for i in range(HEADS // 2):
         col = columns(core * (HEADS // 2) + i)
         state_own[columns(i), :] = tn(k[:, col], v[:, col])
@@ -197,7 +205,7 @@
     shared = [(q_hbm, q), (k_hbm, kx), (v_hbm, vx), (c_hbm, c)]
     for n, (src, dst) in enumerate(shared):
         send(src.at[:, theirs], dst.at[:, ours], 8 + n, sibling)
-    for load in loads[2:]:
+    for load in loads[4:]:
         load.wait()
 
     def inside(h, carry):
@@ -400,7 +408,7 @@
             suffix,
             pltpu.VMEM((2, WIDTH, DH), BF16),
             pltpu.VMEM((2, 2 * NX, 2, TOK), F32),
-            pltpu.SemaphoreType.DMA((8,)),
+            pltpu.SemaphoreType.DMA((10,)),
             pltpu.SemaphoreType.DMA((16,)),
             pltpu.SemaphoreType.DMA((16,)),
         ],

time: 48 us -> 47.6 us (level)
  Pallas kernels: 47.3 us -> 46.8 us
    pallas_call x1, Pallas kernels: 45.2 us -> 44.7 us  [per_device(): pl.pallas_call(kernel, out_shape=[held, held, held_half, held_half, held,...]
where the time goes in v5:
time: 47.6 us; the launch traced here: 47.4 us
  Pallas kernels  46.8 us (98%)
  between operations  0.64 us (1%)
    pallas_call x1, Pallas kernels, per_device(): pl.pallas_call(kernel, out_shape=[held, held, held_half, held_half, held,...  44.7 us
    pallas_call x1, Pallas kernels, per_device(): pl.pallas_call(finish, out_shape=[block] * 4, in_specs=[pl.BlockSpec(memo...  2.07 us

profile of v5, /device:TPU:1, one launch (start us, length us, event | category | flops | bytes accessed | tf_op | source)
XLA Modules:
  0.0 47.4 jit_solution(2654123442495452395)
XLA Ops:
  0.6 44.7 %shard_map.84 = (bf16[512,1024]{1,0:T(8,128)(2,1)S(1)}, bf16[512,1024]{1,0:T(8,128)(2,1)S(1)}, bf16[512,512]{1,0:T(8,128)(2,1)S(1)}, bf16[512,512]{1,0:T(8,128)(...) custom-call(bf16[512,1024]{1,0:T(8,128)(2,1)} %q_hbm.1, ...), custom_call_target="tpu_custom_call" | custom-call | tf_op jit(solution)/shard_map/pallas_call | solution.py:378
  45.4 2.1 %shard_map.85 = (bf16[512,1024]{1,0:T(8,128)(2,1)}, bf16[512,1024]{1,0:T(8,128)(2,1)}, bf16[512,1024]{1,0:T(8,128)(2,1)}, bf16[512,1024]{1,0:T(8,128)(2,1)}) custom-call(bf16[512,1024]{1,0:T(8,128)(2,1)S(1)} %get-tuple-element.13.normed, bf16[512,1024]{1,0:T(8,128)(2,1)S(1)} %get-tuple-element.14.grad_q, bf16[512,512]{1,0:T(8,128)(2,1)S(1)} %get-tuple-element.15.grad_k, ...), custom_call_target="tpu_custom_call" | custom-call | tf_op jit(solution)/shard_map/pallas_call | solution.py:419

commit v6 on v5

--- a/solution.py
+++ b/solution.py
@@ -87,6 +87,7 @@
     chip_scan,
     suffix_out,
     scan,
+    paired,
     stats,
     load_sem,
     send_sem,
@@ -102,9 +103,11 @@
     sign = 1 - 2 * core
     sibling = (twin, hx)
 
+    ys = [lax.rem(chip_y + NY + sign * dy, NY) for dy in range(NY)]
+    zs = [lax.rem(chip_z + NZ + sign * dz, NZ) for dz in range(NZ)]
+
     def chip_at(dy, dz):
-        y = lax.rem(chip_y + NY + sign * dy, NY)
-        return y * NZ + lax.rem(chip_z + NZ + sign * dz, NZ)
+        return ys[dy] * NZ + zs[dz]
 
     offsets = far_first()
     barrier = pltpu.get_barrier_semaphore()
@@ -231,16 +234,20 @@
     for n, (src, dst) in enumerate(shared):
         await_bytes(dst.at[:, theirs], recv_sem.at[8 + n])
     lax.fori_loop(first_other, first_other + HEADS // 2, inside, 0)
+    paired[...] = jnp.zeros_like(paired)
     ahead = scan_end(0)
     scan[0, :HALF, :] = ahead.astype(BF16)
     between = jnp.where(core == 0, state_own[...], state_in[...].astype(F32))
     scan[0, HALF:, :] = (ahead + between).astype(BF16)
+    for h in range(HEADS):
+        side = slice(h % 2 * DH, (h % 2 + 1) * DH)
+        paired[h // 2, side, side] = scan[0, h * DH : (h + 1) * DH, :]
 
     slot = hx * 2 + core
     for b in range(2):
-        for h in range(b * HEADS // 2, (b + 1) * HEADS // 2):
-            col = slice(h * DH, (h + 1) * DH)
-            att[:, col] += nn(q8[:, col], scan[0, col, :])
+        for pair in range(b * HEADS // 4, (b + 1) * HEADS // 4):
+            col = slice(2 * pair * DH, (2 * pair + 2) * DH)
+            att[:, col] += nn(q8[:, col], paired[pair])
         for i in range(TOK // DH):
             rows = slice(i * DH, (i + 1) * DH)
             squares = jnp.zeros((DH, DH), F32)
@@ -339,7 +346,7 @@
 
 
 def finish(normed, grad_q, grad_k, grad_v, k, v, part_k, part_v, suffix, *rest):
-    normed_out, grad_q_out, grad_k_out, grad_v_out, last_k, last_v, sem = rest
+    normed_out, grad_q_out, grad_k_out, grad_v_out, last_k, last_v, paired, sem = rest
     core = lax.rem(lax.axis_index("ctx"), 2)
     ours = pl.ds(pl.multiple_of(core * HALF, HALF), HALF)
     stores = []
@@ -353,17 +360,18 @@
     store(grad_q, grad_q_out)
     store(grad_k, grad_k_out.at[:, ours])
     store(grad_v, grad_v_out.at[:, ours])
+    paired[...] = jnp.zeros_like(paired)
     for i in range(HEADS // 2):
-        to = slice(i * DH, (i + 1) * DH)
-        col = pl.ds(pl.multiple_of((1 - core) * HALF + i * DH, DH), DH)
-        after = suffix[to, :]
-        last_k[:, to] = (part_k[:, col] + nt(v[:, col], after)).astype(BF16)
-        last_v[:, to] = (part_v[:, col] + nn(k[:, col], after)).astype(BF16)
-        if i % 2:
-            pair = pl.ds((i - 1) * DH, 2 * DH)
-            out = pl.ds(pl.multiple_of((1 - core) * HALF + (i - 1) * DH, 2 * DH), 2 * DH)
-            store(last_k.at[:, pair], grad_k_out.at[:, out])
-            store(last_v.at[:, pair], grad_v_out.at[:, out])
+        side = slice(i % 2 * DH, (i % 2 + 1) * DH)
+        paired[i // 2, side, side] = suffix[i * DH : (i + 1) * DH, :]
+    for i in range(HEADS // 4):
+        pair = pl.ds(i * 2 * DH, 2 * DH)
+        col = pl.ds(pl.multiple_of((1 - core) * HALF + i * 2 * DH, 2 * DH), 2 * DH)
+        after = paired[i]
+        last_k[:, pair] = (part_k[:, col] + nt(v[:, col], after)).astype(BF16)
+        store(last_k.at[:, pair], grad_k_out.at[:, col])
+        last_v[:, pair] = (part_v[:, col] + nn(k[:, col], after)).astype(BF16)
+        store(last_v.at[:, pair], grad_v_out.at[:, col])
     for copy in stores:
         copy.wait()
 
@@ -407,6 +415,7 @@
             pieces,
             suffix,
             pltpu.VMEM((2, WIDTH, DH), BF16),
+            pltpu.VMEM((HEADS // 2, 2 * DH, 2 * DH), BF16),
             pltpu.VMEM((2, 2 * NX, 2, TOK), F32),
             pltpu.SemaphoreType.DMA((10,)),
             pltpu.SemaphoreType.DMA((16,)),
@@ -421,7 +430,12 @@
         out_shape=[block] * 4,
         in_specs=[pl.BlockSpec(memory_space=pltpu.VMEM)] * 9,
         out_specs=[pl.BlockSpec(memory_space=pltpu.HBM)] * 4,
-        scratch_shapes=[held_half, held_half, pltpu.SemaphoreType.DMA((4 + HEADS // 2,))],
+        scratch_shapes=[
+            held_half,
+            held_half,
+            pltpu.VMEM((HEADS // 4, 2 * DH, 2 * DH), BF16),
+            pltpu.SemaphoreType.DMA((4 + HEADS // 2,)),
+        ],
         compiler_params=pltpu.CompilerParams(vmem_limit_bytes=16 << 20),
     )(*passed)
 

time: 47.6 us -> 47.6 us (level)
  no operation moved by 1% of the time
where the time goes in v6:
time: 47.6 us; the launch traced here: 47.5 us
  Pallas kernels  46.9 us (99%)
  between operations  0.64 us (1%)
    pallas_call x1, Pallas kernels, per_device(): pl.pallas_call(kernel, out_shape=[held, held, held_half, held_half, held,...  44.7 us
    pallas_call x1, Pallas kernels, per_device(): pl.pallas_call(finish, out_shape=[block] * 4, in_specs=[pl.BlockSpec(memo...  2.11 us

profile of v6, /device:TPU:1, one launch (start us, length us, event | category | flops | bytes accessed | tf_op | source)
XLA Modules:
  0.0 47.5 jit_solution(13215779919561221891)
XLA Ops:
  0.6 44.7 %shard_map.84 = (bf16[512,1024]{1,0:T(8,128)(2,1)S(1)}, bf16[512,1024]{1,0:T(8,128)(2,1)S(1)}, bf16[512,512]{1,0:T(8,128)(2,1)S(1)}, bf16[512,512]{1,0:T(8,128)(...) custom-call(bf16[512,1024]{1,0:T(8,128)(2,1)} %q_hbm.1, ...), custom_call_target="tpu_custom_call" | custom-call | tf_op jit(solution)/shard_map/pallas_call | solution.py:386
  45.4 2.1 %shard_map.85 = (bf16[512,1024]{1,0:T(8,128)(2,1)}, bf16[512,1024]{1,0:T(8,128)(2,1)}, bf16[512,1024]{1,0:T(8,128)(2,1)}, bf16[512,1024]{1,0:T(8,128)(2,1)}) custom-call(bf16[512,1024]{1,0:T(8,128)(2,1)S(1)} %get-tuple-element.13.normed, bf16[512,1024]{1,0:T(8,128)(2,1)S(1)} %get-tuple-element.14.grad_q, bf16[512,512]{1,0:T(8,128)(2,1)S(1)} %get-tuple-element.15.grad_k, ...), custom_call_target="tpu_custom_call" | custom-call | tf_op jit(solution)/shard_map/pallas_call | solution.py:428

commit v7 on v5

--- a/solution.py
+++ b/solution.py
@@ -20,6 +20,7 @@
 PIECE = HALF // CHIPS
 FULL_WIDTH = WIDTH * NX
 CUT = TOK // 2
+SPLIT = 2
 
 
 def far_first():
@@ -349,10 +350,12 @@
         copy.start()
         stores.append(copy)
 
-    store(normed, normed_out)
-    store(grad_q, grad_q_out)
-    store(grad_k, grad_k_out.at[:, ours])
-    store(grad_v, grad_v_out.at[:, ours])
+    for part in range(SPLIT):
+        rows = pl.ds(part * (TOK // SPLIT), TOK // SPLIT)
+        store(normed.at[rows], normed_out.at[rows])
+        store(grad_q.at[rows], grad_q_out.at[rows])
+        store(grad_k.at[rows], grad_k_out.at[rows, ours])
+        store(grad_v.at[rows], grad_v_out.at[rows, ours])
     for i in range(HEADS // 2):
         to = slice(i * DH, (i + 1) * DH)
         col = pl.ds(pl.multiple_of((1 - core) * HALF + i * DH, DH), DH)
@@ -421,7 +424,7 @@
         out_shape=[block] * 4,
         in_specs=[pl.BlockSpec(memory_space=pltpu.VMEM)] * 9,
         out_specs=[pl.BlockSpec(memory_space=pltpu.HBM)] * 4,
-        scratch_shapes=[held_half, held_half, pltpu.SemaphoreType.DMA((4 + HEADS // 2,))],
+        scratch_shapes=[held_half, held_half, pltpu.SemaphoreType.DMA((4 * SPLIT + HEADS // 2,))],
         compiler_params=pltpu.CompilerParams(vmem_limit_bytes=16 << 20),
     )(*passed)
 

time: 47.6 us -> 47.6 us (level)
  no operation moved by 1% of the time
where the time goes in v7:
time: 47.6 us; the launch traced here: 47.5 us
  Pallas kernels  46.8 us (98%)
  between operations  0.64 us (1%)
    pallas_call x1, Pallas kernels, per_device(): pl.pallas_call(kernel, out_shape=[held, held, held_half, held_half, held,...  44.7 us
    pallas_call x1, Pallas kernels, per_device(): pl.pallas_call(finish, out_shape=[block] * 4, in_specs=[pl.BlockSpec(memo...  2.12 us

profile of v7, /device:TPU:1, one launch (start us, length us, event | category | flops | bytes accessed | tf_op | source)
XLA Modules:
  0.0 47.5 jit_solution(13271299349250761581)
XLA Ops:
  0.6 44.7 %shard_map.84 = (bf16[512,1024]{1,0:T(8,128)(2,1)S(1)}, bf16[512,1024]{1,0:T(8,128)(2,1)S(1)}, bf16[512,512]{1,0:T(8,128)(2,1)S(1)}, bf16[512,512]{1,0:T(8,128)(...) custom-call(bf16[512,1024]{1,0:T(8,128)(2,1)} %q_hbm.1, ...), custom_call_target="tpu_custom_call" | custom-call | tf_op jit(solution)/shard_map/pallas_call | solution.py:381
  45.4 2.1 %shard_map.85 = (bf16[512,1024]{1,0:T(8,128)(2,1)}, bf16[512,1024]{1,0:T(8,128)(2,1)}, bf16[512,1024]{1,0:T(8,128)(2,1)}, bf16[512,1024]{1,0:T(8,128)(2,1)}) custom-call(bf16[512,1024]{1,0:T(8,128)(2,1)S(1)} %get-tuple-element.13.normed, bf16[512,1024]{1,0:T(8,128)(2,1)S(1)} %get-tuple-element.14.grad_q, bf16[512,512]{1,0:T(8,128)(2,1)S(1)} %get-tuple-element.15.grad_k, ...), custom_call_target="tpu_custom_call" | custom-call | tf_op jit(solution)/shard_map/pallas_call | solution.py:422
